TPU v7x, 128 devices: a whole 4x4x4 slice. The times are simulated.
128 devices in a mesh: rad: 8 (over y, core), lat: 16 (over x, z).
Axes of the slice: x: 4, y: 4, z: 4, core: 2. Of those that a mesh axis runs over, the one named last changes fastest.
Arguments:
- entropy: bfloat16 [256, 1024, 2, 256], P('lat', None, None, 'rad'), may hold values from -6 to 6
- legendre: bfloat16 [256, 1024, 1024], P('lat', 'rad'), may hold values from -0.1875 to 0.1875
- quad_weights: float32 [1024], replicated, may hold values from 0.5 to 2
- azimuthal_orders: int32 [256], replicated, may hold values from 0 to 1023, as said below
- azimuthal_flow: bfloat16 [3072, 256, 1024], P(None, 'lat', 'rad'), may hold values from -24 to 24
- radial_inverses: bfloat16 [1024, 256, 256], P(('rad', 'lat')), may hold values from -1 to 2
Outputs:
- entropy_next: bfloat16 [256, 1024, 2, 256], P(None, ('rad', 'lat'))
Inputs may be any that keep to these rules, and one draw needn't show every extreme that they name: `azimuthal_orders`: distinct and ascending over the slots; the first is 0 and the last is 1023.
All inputs are finite; a program needn't handle non-finite values.
Results may differ from a plain program's by a relative error of at most 0.0051.
Values may be sent and summed in bfloat16 or wider, within the bound.
A program may use at most 128 MiB of HBM per device.

v0:
```python
import math

import jax
import jax.numpy as jnp
from jax import lax
from jax.sharding import PartitionSpec as P


def azimuth_tables(orders, n_phi, n_deg):
    steps_k = lax.broadcasted_iota(jnp.int32, (n_phi, 1), 0)
    phases = steps_k * orders[None, :] % n_phi
    angles = phases.astype(jnp.float32) * (2.0 * math.pi / n_phi)
    scaled = orders.astype(jnp.float32)[None, :] / n_deg
    sines = jnp.sin(angles)
    cosines = jnp.cos(angles)
    slope_table = jnp.stack([-(scaled * sines), -(scaled * cosines)], axis=2).astype(jnp.bfloat16)
    fourier_table = jnp.stack([cosines, -sines], axis=2).astype(jnp.bfloat16)
    return (slope_table, fourier_table)


def synthesize(order, table, coeffs, block_size):
    n_deg = table.shape[1]
    flattened = coeffs.reshape(n_deg, -1)
    degrees = lax.broadcasted_iota(jnp.int32, (1, block_size), 1)

    def synthesize_add_block(block_index, running):
        lower_row = block_index * block_size
        table_piece = lax.dynamic_slice_in_dim(table, lower_row, block_size, 1)
        table_piece = jnp.where(
            degrees + lower_row >= order, table_piece, jnp.zeros_like(table_piece)
        )
        coeff_rows = lax.dynamic_slice_in_dim(flattened, lower_row, block_size, 0)
        return running + lax.dot_general(
            coeff_rows, table_piece, (((0,), (1,)), ((), ())), preferred_element_type=jnp.float32
        )

    starting = jnp.zeros((flattened.shape[1], table.shape[0]), jnp.float32)
    return lax.fori_loop(order // block_size, n_deg // block_size, synthesize_add_block, starting)


def analyze(order, table, weights, field, coeffs, block_size):
    n_deg = table.shape[1]
    flat_field = field.reshape(-1, table.shape[0])
    degrees = lax.broadcasted_iota(jnp.int32, (1, block_size), 1)

    def analyze_add_block(block_index, running):
        lower_row = block_index * block_size
        table_piece = (
            lax.dynamic_slice_in_dim(table, lower_row, block_size, 1).astype(jnp.float32)
            * weights[:, None]
        )
        table_piece = jnp.where(degrees + lower_row >= order, table_piece, 0.0).astype(jnp.bfloat16)
        product = lax.dot_general(
            table_piece, flat_field, (((0,), (1,)), ((), ())), preferred_element_type=jnp.float32
        )
        current = lax.dynamic_slice_in_dim(running, lower_row, block_size, 0)
        return lax.dynamic_update_slice_in_dim(running, current + product, lower_row, 0)

    starting = coeffs.reshape(n_deg, -1).astype(jnp.float32)
    return lax.fori_loop(order // block_size, n_deg // block_size, analyze_add_block, starting)


def shards(entropy, legendre, quad_weights, azimuthal_orders, azimuthal_flow, radial_inverses):
    rad_count = lax.axis_size("rad")
    lat_count = lax.axis_size("lat")
    rad_pos = lax.axis_index("rad")
    lat_pos = lax.axis_index("lat")
    lat_slots = entropy.shape[0]
    own_slots = lat_slots // rad_count
    n_deg = entropy.shape[1]
    block_size = 128
    own_spec = lax.all_to_all(entropy, "rad", split_axis=0, concat_axis=3, tiled=True)
    own_table = lax.all_to_all(legendre, "rad", split_axis=0, concat_axis=1, tiled=True)
    first_slot = lat_pos * lat_slots + rad_pos * own_slots
    own_orders = lax.dynamic_slice_in_dim(azimuthal_orders, first_slot, own_slots)
    radii = own_spec.shape[3]
    lat_points = own_table.shape[1]
    synthesized = []
    for slot_index in range(own_slots):
        values = synthesize(
            own_orders[slot_index], own_table[slot_index], own_spec[slot_index], block_size
        )
        synthesized.append(values.reshape(2, radii, lat_points))
    grid_values = jnp.stack(synthesized).astype(jnp.bfloat16)
    r_part = radii // lat_count
    t_part = lat_points // rad_count
    points = lax.all_to_all(
        lax.all_to_all(grid_values, "rad", split_axis=3, concat_axis=0, tiled=True),
        "lat",
        split_axis=2,
        concat_axis=0,
        tiled=True,
    )
    n_phi = azimuthal_flow.shape[0]
    band_size = azimuthal_orders.shape[0]
    slope_table, fourier_table = azimuth_tables(azimuthal_orders, n_phi, n_deg)
    flat_points = points.reshape(band_size, 2, r_part * t_part)
    slope = lax.dot_general(
        slope_table, flat_points, (((1, 2), (0, 1)), ((), ())), preferred_element_type=jnp.float32
    )
    forcing = (-azimuthal_flow.reshape(n_phi, -1).astype(jnp.float32) * slope).astype(jnp.bfloat16)
    meridional = lax.dot_general(
        fourier_table, forcing, (((0,), (0,)), ((), ())), preferred_element_type=jnp.float32
    )
    meridional = (2.0 / n_phi * meridional).astype(jnp.bfloat16)
    grouped = meridional.reshape(lat_count, rad_count * own_slots, 2, r_part, t_part)
    returned = lax.all_to_all(
        lax.all_to_all(grouped, "rad", split_axis=1, concat_axis=4, tiled=True),
        "lat",
        split_axis=0,
        concat_axis=3,
        tiled=True,
    )
    own_field = returned.reshape(own_slots, 2, radii, lat_points)
    sides = []
    for slot_index in range(own_slots):
        solved = analyze(
            own_orders[slot_index],
            own_table[slot_index],
            quad_weights,
            own_field[slot_index],
            own_spec[slot_index],
            block_size,
        )
        sides.append(solved.reshape(n_deg, 2, radii))
    right_side = jnp.stack(sides).astype(jnp.bfloat16)
    by_degree = lax.all_to_all(
        lax.all_to_all(right_side, "rad", split_axis=1, concat_axis=0, tiled=True),
        "lat",
        split_axis=1,
        concat_axis=0,
        tiled=True,
    )
    updated = jnp.einsum(
        "mlcs,lrs->mlcr", by_degree, radial_inverses, preferred_element_type=jnp.float32
    )
    return updated.astype(jnp.bfloat16)


def solution(mesh):
    placed = (
        P("lat", None, None, "rad"),
        P("lat", "rad", None),
        P(),
        P(),
        P(None, "lat", "rad"),
        P(("rad", "lat"), None, None),
    )
    return jax.shard_map(
        shards,
        mesh=mesh,
        in_specs=placed,
        out_specs=P(None, ("rad", "lat"), None, None),
        check_vma=False,
    )
```

profile of v0, /device:TPU:1, one launch (start us, length us, event | category | flops | bytes accessed | tf_op | source)
XLA Modules:
  0.0 485.2 jit_solution(12229182493171511481)
XLA Ops:
  0.0 32.6 %all_to_all.132 = bf16[16,1024,2,32]{1,3,2,0:T(8,128)(2,1)S(1)} all-to-all(bf16[16,1024,2,32]{1,3,2,0:T(8,128)(2,1)} %param.14), channel_id=1, replica_groups=mesh['rad'=8,'lat'=16] {'rad'}, dimensions={0} | all-to-all | bytes 4194304 | tf_op jit(solution)/shard_map/all_to_all | solution.py:72
  32.6 5.6 %all-to-all-start.1 = ((bf16[16,128,1024]{2,1,0:T(8,128)(2,1)}), bf16[16,128,1024]{2,1,0:T(8,128)(2,1)}, u32[]{:S(2)}, u32[]{:S(2)}) async-start(bf16[16,128,1024]{2,1,0:T(8,128)(2,1)} %param.15), calls=%async_computation.1 | async-start | bytes 8388608 | tf_op jit(solution)/shard_map/all_to_all | solution.py:73
  46.2 40.9 %all-to-all-done.1 = bf16[16,128,1024]{2,1,0:T(8,128)(2,1)} async-done(((bf16[16,128,1024]{2,1,0:T(8,128)(2,1)}), bf16[16,128,1024]{2,1,0:T(8,128)(2,1)}, u32[]{:S(2)}, u32[]{:S(2)}) %all-to-all-start.1) | async-done | bytes 4194336 | tf_op jit(solution)/shard_map/all_to_all | solution.py:73
  92.5 17.1 %while.44 = (s32[]{:T(128)}, f32[512,1024]{1,0:T(8,128)S(1)}, bf16[1024,512]{0,1:T(8,128)(2,1)}, s32[]{:T(128)}, bf16[1024,1024]{1,0:T(8,128)(2,1)}, /*index=5*/s32[]{:T(128)}, s32[]{:T(128)}, s32[]{:T(128)}, s32[]{:T(128)}) while((s32[]{:T(128)}, f32[512,1024]{1,0:T(8,128)S(1)}, bf16[1024,512]{0,1:T(8,128)(2,1)}, s32[]{:T(128)}, ...), condition=%wide.region_1.2_spmd.clone, body=%wide.region_0.1_spmd.clone.sunk | while | flops 134873344 | bytes 4588947 | solution.py:38
  111.0 17.1 %while.45 = (s32[]{:T(128)}, f32[512,1024]{1,0:T(8,128)S(1)}, bf16[1024,512]{0,1:T(8,128)(2,1)}, s32[]{:T(128)}, bf16[1024,1024]{1,0:T(8,128)(2,1)}, /*index=5*/s32[]{:T(128)}, s32[]{:T(128)}, s32[]{:T(128)}, s32[]{:T(128)}) while((s32[]{:T(128)}, f32[512,1024]{1,0:T(8,128)S(1)}, bf16[1024,512]{0,1:T(8,128)(2,1)}, s32[]{:T(128)}, ...), condition=%wide.region_3.4_spmd.clone, body=%wide.region_2.3_spmd.clone.sunk | while | flops 134873344 | bytes 4588947 | solution.py:38
  129.5 4.0 copy.81
  133.5 4.4 all-to-all-start.2
  137.9 26.3 %all-to-all-done.2 = bf16[2,2,256,1024]{2,1,0,3:T(2,128)(2,1)S(1)} async-done(((bf16[2,2,256,1024]{2,1,0,3:T(2,128)(2,1)}), bf16[2,2,256,1024]{2,1,0,3:T(2,128)(2,1)S(1)}, u32[]{:S(2)}, u32[]{:S(2)}) %all-to-all-start.2) | async-done | bytes 2097184 | tf_op jit(solution)/shard_map/all_to_all | solution.py:88
  165.8 3.0 copy.83
  168.9 3.5 copy.84
  172.4 3.9 all-to-all-start.3
  176.3 15.4 %negate_convert_fusion.1 = (bf16[3072,256,1]{1,0,2:T(8,128)(2,1)}, bf16[3072,256,1]{1,0,2:T(8,128)(2,1)}, bf16[3072,256,1]{1,0,2:T(8,128)(2,1)}, bf16[3072,256,1]{1,0,2:T(8,128)(2,1)}) fusion(f32[256]{0:T(256)S(1)} %convert_multiply_fusion, s32[256]{0:T(256)S(1)} %copy-done.5), kind=kLoop, calls=%fused_computation.65 | loop fusion | flops 14155776 | bytes 6293504 | tf_op jit(solution)/shard_map/convert.8
  191.6 13.9 %convert_negate_fusion = f32[3072,16,128]{2,1,0:T(8,128)} fusion(bf16[3072,16,128]{2,1,0:T(8,128)(2,1)} %param.18), kind=kLoop, calls=%fused_computation.50 | loop fusion | flops 12582912 | bytes 37748736 | tf_op jit(solution)/shard_map/neg | solution.py:101
  210.5 26.2 %multiply_convert_fusion = bf16[256,2,2048]{2,0,1:T(8,128)(2,1)} fusion(bf16[256,2,2048]{2,0,1:T(8,128)(2,1)S(1)} %reshape.238, f32[384,8,16,128]{3,2,1,0:T(8,128)} %bitcast.116, bf16[3072,256,1]{1,0,2:T(8,128)(2,1)} %get-tuple-element.361, bf16[3072,256,1]{1,0,2:T(8,128)(2,1)} %get-tuple-element.362, bf16[3072,256,1]{1,0,2:T(8,128)(2,1)} %get-tuple-element.360, ...), kind=kOutput, calls=%fused_computation.55 | convolution fusion | flops 12902727680 | bytes 35651584 | tf_op jit(solution)/shard_map/dot_general | solution.py:102
  239.5 30.8 %all_to_all.133 = bf16[16,16,2,16,128]{4,3,0,2,1:T(8,128)(2,1)S(1)} all-to-all(bf16[16,16,2,16,128]{4,3,0,2,1:T(8,128)(2,1)S(1)} %copy.87), channel_id=1, replica_groups=mesh['rad'=8,'lat'=16] {'rad'}, dimensions={1} | all-to-all | bytes 4194304 | tf_op jit(solution)/shard_map/all_to_all | solution.py:108
  275.1 5.7 %all-to-all-start.5 = ((bf16[16,2,2,16,1024]{4,3,2,1,0:T(8,128)(2,1)}), bf16[16,2,2,16,1024]{4,3,2,1,0:T(8,128)(2,1)S(1)}, u32[]{:S(2)}, u32[]{:S(2)}) async-start(bf16[16,2,2,16,1024]{4,3,2,1,0:T(8,128)(2,1)} %all_to_all.112), calls=%async_computation.5 | async-start | bytes 4194304 | tf_op jit(solution)/shard_map/all_to_all | solution.py:107
  280.8 2.9 bitcast_convert_fusion.1
  285.3 21.2 %all-to-all-done.5 = bf16[16,2,2,16,1024]{4,3,2,1,0:T(8,128)(2,1)S(1)} async-done(((bf16[16,2,2,16,1024]{4,3,2,1,0:T(8,128)(2,1)}), bf16[16,2,2,16,1024]{4,3,2,1,0:T(8,128)(2,1)S(1)}, u32[]{:S(2)}, u32[]{:S(2)}) %all-to-all-start.5) | async-done | bytes 2097184 | tf_op jit(solution)/shard_map/all_to_all | solution.py:107
  307.4 61.1 %while.46 = (s32[]{:T(128)}, f32[1024,512]{0,1:T(8,128)}, s32[]{:T(128)}, bf16[1024,1024]{1,0:T(8,128)(2,1)}, f32[1024]{0:T(1024)S(1)}, /*index=5*/bf16[512,1024...) while((s32[]{:T(128)}, f32[1024,512]{0,1:T(8,128)}, s32[]{:T(128)}, ...), condition=%wide.region_5.6_spmd.clone, body=%wide.region_4.5_spmd.clone.sunk | while | flops 134807808 | bytes 3936679 | solution.py:60
  371.2 34.5 %while.47 = (s32[]{:T(128)}, f32[1024,512]{0,1:T(8,128)}, s32[]{:T(128)}, bf16[1024,1024]{1,0:T(8,128)(2,1)}, f32[1024]{0:T(1024)S(1)}, /*index=5*/bf16[512,1024...) while((s32[]{:T(128)}, f32[1024,512]{0,1:T(8,128)}, s32[]{:T(128)}, ...), condition=%wide.region_7.8_spmd.clone, body=%wide.region_6.7_spmd.clone.sunk | while | flops 134807808 | bytes 3936679 | solution.py:60
  407.8 4.0 copy.94
  411.8 35.2 %all_to_all.134 = bf16[2,1024,2,256]{3,2,0,1:T(2,128)(2,1)S(1)} all-to-all(bf16[2,1024,2,256]{3,2,0,1:T(2,128)(2,1)} %copy.94), channel_id=1, replica_groups=mesh['rad'=8,'lat'=16] {'rad'}, dimensions={1} | all-to-all | bytes 4194304 | tf_op jit(solution)/shard_map/all_to_all | solution.py:128
  449.6 29.0 %all_to_all.135 = bf16[16,128,2,256]{3,2,0,1:T(2,128)(2,1)S(1)} all-to-all(bf16[16,128,2,256]{3,2,0,1:T(2,128)(2,1)S(1)} %copy.97), channel_id=1, replica_groups=mesh['rad'=8,'lat'=16] {'lat'}, dimensions={1} | all-to-all | bytes 4194304 | tf_op jit(solution)/shard_map/all_to_all | solution.py:127
  481.7 3.5 copy.100
  (173 shorter events, 167.0 us)
Async XLA Ops:
  0.0 481.0 %copy-start = (bf16[8,256,256]{2,1,0:T(8,128)(2,1)S(1)}, bf16[8,256,256]{2,1,0:T(8,128)(2,1)}, u32[]{:S(2)}) copy-start(bf16[8,256,256]{2,1,0:T(8,128)(2,1)} %param.19) | copy-start | bytes 3145732
  32.6 5.6 %copy-start.5 = (s32[256]{0:T(256)S(1)}, s32[256]{0:T(256)}, u32[]{:S(2)}) copy-start(s32[256]{0:T(256)} %param.17) | copy-start | bytes 3076
  32.6 54.5 %all-to-all-start.1 = ((bf16[16,128,1024]{2,1,0:T(8,128)(2,1)}), bf16[16,128,1024]{2,1,0:T(8,128)(2,1)}, u32[]{:S(2)}, u32[]{:S(2)}) async-start(bf16[16,128,1024]{2,1,0:T(8,128)(2,1)} %param.15), calls=%async_computation.1 | async-start | bytes 8388608 | tf_op jit(solution)/shard_map/all_to_all | solution.py:73
  128.0 1.2 copy-start.3
  133.5 30.7 %all-to-all-start.2 = ((bf16[2,2,256,1024]{2,1,0,3:T(2,128)(2,1)}), bf16[2,2,256,1024]{2,1,0,3:T(2,128)(2,1)S(1)}, u32[]{:S(2)}, u32[]{:S(2)}) async-start(bf16[2,2,256,1024]{2,1,0,3:T(2,128)(2,1)} %copy.81), calls=%async_computation.2 | async-start | bytes 4194304 | tf_op jit(solution)/shard_map/all_to_all | solution.py:88
  172.4 33.1 %all-to-all-start.3 = ((bf16[16,2,256,128]{3,1,0,2:T(2,128)(2,1)}), bf16[16,2,256,128]{3,1,0,2:T(2,128)(2,1)S(1)}, u32[]{:S(2)}, u32[]{:S(2)}) async-start(bf16[16,2,256,128]{3,1,0,2:T(2,128)(2,1)} %copy.84), calls=%async_computation.3 | async-start | bytes 4194304 | tf_op jit(solution)/shard_map/all_to_all | solution.py:87
  275.1 31.4 %all-to-all-start.5 = ((bf16[16,2,2,16,1024]{4,3,2,1,0:T(8,128)(2,1)}), bf16[16,2,2,16,1024]{4,3,2,1,0:T(8,128)(2,1)S(1)}, u32[]{:S(2)}, u32[]{:S(2)}) async-start(bf16[16,2,2,16,1024]{4,3,2,1,0:T(8,128)(2,1)} %all_to_all.112), calls=%async_computation.5 | async-start | bytes 4194304 | tf_op jit(solution)/shard_map/all_to_all | solution.py:107
  280.8 2.9 copy-start.1
  306.7 0.7 copy-start.4
  405.7 1.9 copy-start.2
where the time goes:
time: 491 us; the launch traced here: 485 us
  blocking collectives  128 us (26%)
  local copies, waits for them, and re-layouts  100 us (20%)
  waiting for transfers between devices  88.5 us (18%)
  matrix products  83.1 us (17%)
  other arithmetic  60 us (12%)
  starting transfers between devices  19.6 us (4%)
  between operations  5.22 us (1%)
    all_to_all x1, waiting for transfers between devices, shards(): lax.all_to_all(legendre, 'rad', split_axis=0, concat_axis=1, tiled=True)  40.9 us
    all_to_all x1, blocking collectives, shards(): lax.all_to_all(right_side, 'rad', split_axis=1, concat_axis=0, tiled=True)  35.2 us
    dot_general x16, matrix products, analyze_add_block(): lax.dot_general(table_piece, flat_field, (((0,), (1,)), ((), ())), prefer...  32.7 us
    all_to_all x1, blocking collectives, shards(): lax.all_to_all(entropy, 'rad', split_axis=0, concat_axis=3, tiled=True)  32.6 us
    dynamic_slice x32, local copies, waits for them, and re-layouts, analyze_add_block(): current = lax.dynamic_slice_in_dim(running, lower_row, block_size, 0)  30.9 us
    all_to_all x1, blocking collectives, shards(): lax.all_to_all(grouped, 'rad', split_axis=1, concat_axis=4, tiled=True)  30.8 us
    all_to_all x1, blocking collectives, shards(): lax.all_to_all(lax.all_to_all(right_side, 'rad', split_axis=1, concat_axi...  29 us
    all_to_all x1, waiting for transfers between devices, shards(): lax.all_to_all(grid_values, 'rad', split_axis=3, concat_axis=0, tiled=True)  26.3 us
  transfers between devices with their start and end apart: 4, of which 3 were waited for; matrix products, arithmetic and copies ran while one was open for 8% of the time, Pallas kernels for 0%

commit v1 on v0

v1 whole, which is shorter than its diff:
```python
import math

import jax
import jax.numpy as jnp
from jax import lax
from jax.experimental import pallas as pl
from jax.experimental.pallas import tpu as pltpu
from jax.sharding import PartitionSpec as P

MESH = pl.DeviceIdType.MESH
F32, BF16 = jnp.float32, jnp.bfloat16
N_DEG = 1024
N_PHI = 3072
PEERS = 32
NT = (((1,), (1,)), ((), ()))
KB = 512


def wait_bytes(ref, sem):
    pltpu.make_async_copy(ref, ref, sem).wait()


def kernel(
    ent, leg, qw, orders, ta, tb, scaled, ua, ub, flow, out,
    ef, lg, wt, slope_t, fourier_t, fl, gsend, grecv, msend, mrecv, mx, wide, macc,
    r1send, r1recv, r2send, r2recv, fsend,
    ag_send, ag_recv, lg_send, lg_recv, fl_sem, g_send, g_recv, m_send, m_recv,
    r1_ssem, r1_rsem, r2_ssem, r2_rsem, f_send, f_recv,
):
    rad = lax.axis_index("rad")
    lat = lax.axis_index("lat")
    y, c = rad // 2, rad % 2
    me = 2 * lat + c
    up, down, across = (y + 1) % 4, (y + 3) % 4, (y + 2) % 4

    def place(index):
        return (2 * y + index % 2, index // 2)

    def flow_copy(step, buf):
        return pltpu.make_async_copy(flow.at[pl.ds(2 * step, 2)], fl.at[buf], fl_sem.at[buf])

    flow_copy(0, 0).start()
    flow_copy(1, 1).start()

    barrier = pltpu.get_barrier_semaphore()

    def greet(offset, carry):
        pl.semaphore_signal(
            barrier, inc=1, device_id=place((me + offset) % PEERS), device_id_type=MESH
        )
        return carry

    lax.fori_loop(1, PEERS, greet, 0)
    for row in (up, down):
        for core in range(2):
            pl.semaphore_signal(
                barrier, inc=1, device_id=(2 * row + core, lat), device_id_type=MESH
            )
    pl.semaphore_wait(barrier, PEERS - 1 + 4)

    def remote(src, dst, send_sem, recv_sem, device):
        pltpu.make_async_remote_copy(
            src_ref=src, dst_ref=dst, send_sem=send_sem, recv_sem=recv_sem,
            device_id=device, device_id_type=MESH,
        ).start()

    def all_to_all(source, target, send_sem, recv_sem):
        pltpu.make_async_copy(source(me), target, recv_sem).start()

        def send(offset, carry):
            dest = (me + offset) % PEERS
            remote(source(dest), target, send_sem, recv_sem, place(dest))
            return carry

        lax.fori_loop(1, PEERS, send, 0)

    def gather_direct(j):
        for row in (up, down):
            for core in range(2):
                remote(
                    ent.at[j, pl.ds(8 * core, 8)], ef.at[j, rad],
                    ag_send.at[j], ag_recv.at[j, rad], (2 * row + core, lat),
                )
        remote(
            ent.at[j, pl.ds(8 * (1 - c), 8)], ef.at[j, rad],
            ag_send.at[j], ag_recv.at[j, rad], (2 * y + 1 - c, lat),
        )
        pltpu.make_async_copy(ent.at[j, pl.ds(8 * c, 8)], ef.at[j, rad], ag_recv.at[j, rad]).start()

    def gather_wait(j, block):
        wait_bytes(ef.at[j, block], ag_recv.at[j, block])

    def gather_forward(j):
        for block, row in ((2 * down, up), (2 * up + 1, down)):
            gather_wait(j, block)
            remote(
                ef.at[j, block], ef.at[j, block],
                ag_send.at[j], ag_recv.at[j, block], (2 * row + c, lat),
            )

    def gather_rest(j):
        for block in (rad, 2 * y + 1 - c, 2 * down + 1, 2 * up, 2 * across, 2 * across + 1):
            gather_wait(j, block)

    def slope_rows(a, carry):
        cos_a, sin_a = ta[0, pl.ds(a, 1), :], ta[1, pl.ds(a, 1), :]
        sines = sin_a * tb[0] + cos_a * tb[1]
        slope_t[pl.ds(pl.multiple_of(64 * a, 64), 64), :] = (-(scaled[...] * sines)).astype(BF16)
        return carry

    def fourier_rows(block, carry):
        rows = pl.ds(pl.multiple_of(64 * block, 64), 64)
        cos_b, sin_b = ub[0, rows, :], ub[1, rows, :]
        for a in range(N_PHI // 128):
            cos_a, sin_a = ua[0, rows, a : a + 1], ua[1, rows, a : a + 1]
            fourier_t[rows, 128 * a : 128 * a + 128] = (cos_a * cos_b - sin_a * sin_b).astype(BF16)
        return carry

    def tables(slot, carry):
        order = orders[16 * lat + 8 * c + slot]
        table = lg[slot]
        degrees = lax.broadcasted_iota(jnp.int32, table.shape, 1)
        lg[slot] = jnp.where(degrees >= order, table, jnp.zeros_like(table))
        turned = jnp.transpose(table.astype(F32))
        weighted = turned * qw[pl.ds(y, 1), :]
        degrees = lax.broadcasted_iota(jnp.int32, turned.shape, 0)
        wt[slot] = jnp.where(degrees >= order, weighted, 0.0).astype(BF16)
        return carry

    def synthesize(j):
        def one(slot, carry):
            coeffs = ef[j, :, slot].reshape(256, N_DEG)
            values = lax.dot_general(coeffs, lg[slot], NT, preferred_element_type=F32)
            for p in range(16):
                for part in range(2):
                    at = 32 * (p // 2) + 16 * part + 8 * (p % 2)
                    for core in range(2):
                        wide[2 * p + core, pl.ds(8 * part + slot, 8, stride=16), :] = values[
                            at : at + 8, 128 * core : 128 * core + 128
                        ]
            return carry

        lax.fori_loop(0, 8, one, 0)

        def pack(dest, carry):
            gsend[j, dest] = wide[dest].astype(BF16).reshape(8, 16, 128)
            return carry

        lax.fori_loop(0, PEERS, pack, 0)
        all_to_all(
            lambda dest: gsend.at[j, dest], grecv.at[j, :, pl.ds(16 * me, 16), :],
            g_send.at[j], g_recv.at[j],
        )

    def grid(j):
        wait_bytes(grecv.at[j], g_recv.at[j])

        def pair(ip, carry):
            step = 4 * j + ip
            buf = ip % 2
            flow_copy(step, buf).wait()
            macc[...] = jnp.zeros_like(macc)

            def longitudes(kb, inner):
                rows = pl.ds(pl.multiple_of(KB * kb, KB), KB)
                points = jnp.concatenate([grecv[j, 2 * ip], grecv[j, 2 * ip + 1]], axis=1)
                slope = jnp.dot(slope_t[rows, :], points, preferred_element_type=F32)
                speed = jnp.concatenate([fl[buf, 0, rows, :], fl[buf, 1, rows, :]], axis=1)
                forcing = (-speed.astype(F32) * slope).astype(BF16)
                macc[...] += jnp.dot(fourier_t[:, rows], forcing, preferred_element_type=F32)
                return inner

            lax.fori_loop(0, N_PHI // KB, longitudes, 0)

            @pl.when(step < 6)
            def _():
                flow_copy(step + 2, buf).start()

            done = (macc[...] * (2.0 / N_PHI)).astype(BF16)
            for half in range(2):
                msend[j, :, 2 * ip + half] = done[:, 128 * half : 128 * half + 128].reshape(
                    PEERS, 16, 128
                )
            return carry

        lax.fori_loop(0, 4, pair, 0)
        all_to_all(
            lambda dest: msend.at[j, dest], mrecv.at[j, me], m_send.at[j], m_recv.at[j]
        )

    def arrange(j):
        wait_bytes(mrecv.at[j], m_recv.at[j])

        def unpack(src, carry):
            wide[src] = mrecv[j, src].reshape(128, 128).astype(F32)
            return carry

        lax.fori_loop(0, PEERS, unpack, 0)

        def one(slot, carry):
            for part in range(2):
                for p in range(0, 16, 2):
                    tiles = [
                        [
                            wide[2 * (p + q) + core, pl.ds(8 * part + slot, 8, stride=16), :]
                            for core in range(2)
                        ]
                        for q in range(2)
                    ]
                    block = jnp.concatenate(
                        [jnp.concatenate(pieces, axis=1) for pieces in tiles], axis=0
                    )
                    at = 128 * part + 8 * p
                    mx[j, slot, at : at + 16, :] = block.astype(BF16)
            return carry

        lax.fori_loop(0, 8, one, 0)

    def partial(j, slot, quarter):
        rows = pl.ds(pl.multiple_of(256 * quarter, 256), 256)
        return lax.dot_general(wt[slot, rows, :], mx[j, slot], NT, preferred_element_type=F32)

    def reduce_first(j):
        def far(slot, carry):
            r1send[j, slot] = partial(j, slot, across).astype(BF16)
            return carry

        for half, row in ((0, up), (1, down)):
            lax.fori_loop(4 * half, 4 * half + 4, far, 0)
            span = pl.ds(4 * half, 4)
            remote(
                r1send.at[j, span], r1recv.at[j, span],
                r1_ssem.at[j], r1_rsem.at[j, half], (2 * row + c, lat),
            )
        for way, row, half in ((0, up, 1), (1, down, 0)):

            def near(slot, carry):
                r2send[j, way, slot] = partial(j, slot, row).astype(BF16)
                return carry

            lax.fori_loop(4 * half, 4 * half + 4, near, 0)
            reduce_send(j, way, row, half)

    def reduce_send(j, way, row, half):
        span = pl.ds(4 * half, 4)
        remote(
            r2send.at[j, way, span], r2recv.at[j, way, span],
            r2_ssem.at[j], r2_rsem.at[j, way, half], (2 * row + c, lat),
        )

    def reduce_second(j):
        for way, row, half in ((0, up, 0), (1, down, 1)):
            span = pl.ds(4 * half, 4)
            wait_bytes(r1recv.at[j, span], r1_rsem.at[j, half])

            def near(slot, carry):
                total = partial(j, slot, row) + r1recv[j, slot].astype(F32)
                r2send[j, way, slot] = total.astype(BF16)
                return carry

            lax.fori_loop(4 * half, 4 * half + 4, near, 0)
            reduce_send(j, way, row, half)

    def finish(j):
        for way in range(2):
            for half in range(2):
                span = pl.ds(4 * half, 4)
                wait_bytes(r2recv.at[j, way, span], r2_rsem.at[j, way, half])
        lanes = pl.ds(pl.multiple_of(256 * y, 256), 256)
        eye = (
            lax.broadcasted_iota(jnp.int32, (256, 256), 0)
            == lax.broadcasted_iota(jnp.int32, (256, 256), 1)
        ).astype(F32).astype(BF16)

        def pair(index, carry):
            sides = []
            for u in range(2):
                slot = 2 * index + u
                own = ef[j, :, slot, :, lanes].reshape(8, 2, 16, 256)
                own = jnp.concatenate([own[:, 0], own[:, 1]], axis=0).reshape(256, 256)
                total = partial(j, slot, y) + lax.dot_general(
                    eye, own, NT, preferred_element_type=F32
                )
                total += r2recv[j, 0, slot].astype(F32) + r2recv[j, 1, slot].astype(F32)
                sides.append(total.reshape(PEERS, 8, 256))
            both = jnp.concatenate(sides, axis=1).astype(BF16)
            fsend[j, :, pl.ds(pl.multiple_of(16 * index, 16), 16), :] = both
            return carry

        lax.fori_loop(0, 4, pair, 0)
        all_to_all(
            lambda dest: fsend.at[j, 16 * (dest % 2) + dest // 2], out.at[j, me],
            f_send.at[j], f_recv.at[j],
        )

    gather_direct(0)
    mine = pl.ds(pl.multiple_of(128 * c, 128), 128)
    remote(
        leg.at[pl.ds(8 * (1 - c), 8)], lg.at[:, mine, :], lg_send, lg_recv, (2 * y + 1 - c, lat)
    )
    pltpu.make_async_copy(leg.at[pl.ds(8 * c, 8)], lg.at[:, mine, :], lg_recv).start()
    lax.fori_loop(0, N_PHI // 64, slope_rows, 0)
    gather_forward(0)
    gather_direct(1)
    lax.fori_loop(0, 8, fourier_rows, 0)
    wait_bytes(lg, lg_recv)
    lax.fori_loop(0, 8, tables, 0)
    gather_rest(0)
    synthesize(0)
    gather_forward(1)
    grid(0)
    gather_rest(1)
    synthesize(1)
    arrange(0)
    reduce_first(0)
    grid(1)
    reduce_second(0)
    arrange(1)
    reduce_first(1)
    finish(0)
    reduce_second(1)
    finish(1)
    for j in range(2):
        wait_bytes(out.at[j], f_recv.at[j])
    for j in range(2):
        wait_bytes(ef.at[j, pl.ds(0, 7)], ag_send.at[j])
        wait_bytes(gsend.at[j, pl.ds(0, PEERS - 1)], g_send.at[j])
        wait_bytes(msend.at[j, pl.ds(0, PEERS - 1)], m_send.at[j])
        wait_bytes(r1send.at[j], r1_ssem.at[j])
        wait_bytes(r2send.at[j], r2_ssem.at[j])
        wait_bytes(fsend.at[j, pl.ds(0, PEERS - 1)], f_send.at[j])
    wait_bytes(lg.at[:, pl.ds(0, 128), :], lg_send)


def waves(phases):
    angles = phases.astype(F32) * (2.0 * math.pi / N_PHI)
    return jnp.stack([jnp.cos(angles), jnp.sin(angles)])


def shards(entropy, legendre, quad_weights, azimuthal_orders, azimuthal_flow, radial_inverses):
    ent = jnp.transpose(entropy, (0, 2, 3, 1)).reshape(16, 2, 2, 2, 8, N_DEG)
    ent = jnp.transpose(ent, (3, 0, 1, 2, 4, 5)).reshape(2, 16, 32, N_DEG)
    flow = jnp.transpose(azimuthal_flow, (1, 0, 2))
    m = jnp.broadcast_to(azimuthal_orders.reshape(PEERS, 1, 8), (PEERS, 2, 8)).reshape(512)
    quarter = jnp.broadcast_to(
        (jnp.arange(2, dtype=jnp.int32) * (N_PHI // 4)).reshape(1, 2, 1), (PEERS, 2, 8)
    ).reshape(512)
    steps = lambda n: jnp.arange(n, dtype=jnp.int32)
    ta = waves((steps(48)[:, None] * 64 * m[None, :] + quarter[None, :]) % N_PHI)
    tb = waves((steps(64)[:, None] * m[None, :]) % N_PHI)
    ua = waves((steps(24)[None, :] * 128 * m[:, None] + quarter[:, None]) % N_PHI)
    ub = waves((steps(128)[None, :] * m[:, None]) % N_PHI)
    scaled = (m.astype(F32) / N_DEG).reshape(1, 512)
    hbm = pl.BlockSpec(memory_space=pl.ANY)
    vmem = pl.BlockSpec(memory_space=pltpu.VMEM)
    smem = pl.BlockSpec(memory_space=pltpu.SMEM)
    dma = pltpu.SemaphoreType.DMA
    received = pl.pallas_call(
        kernel,
        out_shape=jax.ShapeDtypeStruct((2, PEERS, 64, 256), BF16),
        in_specs=[hbm, hbm, vmem, smem, vmem, vmem, vmem, vmem, vmem, hbm],
        out_specs=hbm,
        scratch_shapes=[
            pltpu.VMEM((2, 8, 8, 32, N_DEG), BF16),
            pltpu.VMEM((8, 256, N_DEG), BF16),
            pltpu.VMEM((8, N_DEG, 256), BF16),
            pltpu.VMEM((N_PHI, 512), BF16),
            pltpu.VMEM((512, N_PHI), BF16),
            pltpu.VMEM((2, 2, N_PHI, 128), BF16),
            pltpu.VMEM((2, PEERS, 8, 16, 128), BF16),
            pltpu.VMEM((2, 8, 512, 128), BF16),
            pltpu.VMEM((2, PEERS, 8, 16, 128), BF16),
            pltpu.VMEM((2, PEERS, 8, 16, 128), BF16),
            pltpu.VMEM((2, 8, 256, 256), BF16),
            pltpu.VMEM((PEERS, 128, 128), F32),
            pltpu.VMEM((512, 256), F32),
            pltpu.VMEM((2, 8, 256, 256), BF16),
            pltpu.VMEM((2, 8, 256, 256), BF16),
            pltpu.VMEM((2, 2, 8, 256, 256), BF16),
            pltpu.VMEM((2, 2, 8, 256, 256), BF16),
            pltpu.VMEM((2, PEERS, 64, 256), BF16),
            dma((2,)), dma((2, 8)), dma, dma, dma((2,)),
            dma((2,)), dma((2,)), dma((2,)), dma((2,)),
            dma((2,)), dma((2, 2)), dma((2,)), dma((2, 2, 2)), dma((2,)), dma((2,)),
        ],
        compiler_params=pltpu.CompilerParams(
            collective_id=0, has_side_effects=True, vmem_limit_bytes=62 * 1024 * 1024
        ),
        cost_estimate=pl.CostEstimate(
            flops=17_000_000_000, bytes_accessed=24_000_000, transcendentals=0
        ),
    )(ent, legendre, quad_weights.reshape(4, 256), azimuthal_orders, ta, tb, scaled, ua, ub, flow)
    sides = received.reshape(2, 256, 8, 2, 128)
    inverses = jnp.transpose(radial_inverses.reshape(8, 256, 16, 2, 8), (0, 3, 2, 4, 1))
    inverses = inverses.reshape(8, 2, 128, 256)
    updated = jnp.einsum("jslcq,ljqr->slcr", sides, inverses, preferred_element_type=F32)
    return updated.astype(BF16)


def solution(mesh):
    placed = (
        P("lat", None, None, "rad"),
        P("lat", "rad", None),
        P(),
        P(),
        P(None, "lat", "rad"),
        P(("rad", "lat"), None, None),
    )
    return jax.shard_map(
        shards,
        mesh=mesh,
        in_specs=placed,
        out_specs=P(None, ("rad", "lat"), None, None),
        check_vma=False,
    )
```

time: 491 us -> 227 us (0.46); the launches traced: 485 us -> 227 us
  Pallas kernels: 0 us -> 200 us
  blocking collectives: 128 us -> 0 us
  waiting for transfers between devices: 88.5 us -> 0 us
  matrix products: 83.1 us -> 2.32 us
  local copies, waits for them, and re-layouts: 100 us -> 20.5 us
  other arithmetic: 60 us -> 4.72 us
  starting transfers between devices: 19.6 us -> 0 us
  between operations: 5.22 us -> 0.08 us
    pallas_call x0 -> x1, Pallas kernels: none -> 200 us  [shards(): pl.pallas_call(kernel, out_shape=jax.ShapeDtypeStruct((2, PEERS, 64, 256)...]
    all_to_all x4 -> x0, blocking collectives: 128 us -> none  [the longest x1 35.2 us: shards(): lax.all_to_all(right_side, 'rad', split_axis=1, concat_axis=0, tiled=True)]
    all_to_all x4 -> x0, waiting for transfers between devices: 88.5 us -> none  [the longest x1 40.9 us: shards(): lax.all_to_all(legendre, 'rad', split_axis=0, concat_axis=1, tiled=True)]
    dot_general x34 -> x1, matrix products: 83.1 us -> 2.32 us  [shards(): jnp.einsum('jslcq,ljqr->slcr', sides, inverses, preferred_element_type=F32)]
    dynamic_slice x33 -> x0, local copies, waits for them, and re-layouts: 30.9 us -> none  [the longest x32 30.9 us: analyze_add_block(): current = lax.dynamic_slice_in_dim(running, lower_row, block_size, 0)]
    all_to_all x13 -> x0, local copies, waits for them, and re-layouts: 22.8 us -> none  [the longest x3 8.12 us: shards(): lax.all_to_all(grid_values, 'rad', split_axis=3, concat_axis=0, tiled=True)]
    dynamic_update_slice x32 -> x0, local copies, waits for them, and re-layouts: 21.6 us -> none  [analyze_add_block(): lax.dynamic_update_slice_in_dim(running, current + product, lower_row, 0)]
    ge x32 -> x0, other arithmetic: 20.1 us -> none  [the longest x16 10 us: analyze_add_block(): degrees + lower_row >= order]
  transfers between devices with their start and end apart: 4 -> 0, of which waited for: 3 -> 0; matrix products, arithmetic and copies ran while one was open for 8% -> 0% of each run, Pallas kernels for 0% -> 0%
where the time goes in v1:
time: 227 us
  Pallas kernels  200 us (88%)
  local copies, waits for them, and re-layouts  20.5 us (9%)
  other arithmetic  4.72 us (2%)
  matrix products  2.32 us (1%)
    pallas_call x1, Pallas kernels, shards(): pl.pallas_call(kernel, out_shape=jax.ShapeDtypeStruct((2, PEERS, 64, 256)...  200 us
    unnamed x8, local copies, waits for them, and re-layouts  12.1 us

profile of v1, /device:TPU:1, one launch (start us, length us, event | category | flops | bytes accessed | tf_op | source)
XLA Modules:
  0.0 227.2 jit_solution(17190747819797836843)
XLA Ops:
  0.0 0.8 broadcast_in_dim.20
  0.8 0.1 mul.197
  0.9 0.1 broadcast_in_dim.22
  1.0 0.1 add.110
  1.1 0.3 fusion.32
  1.4 1.0 copy.25.ua
  2.4 0.5 fusion.25
  2.9 0.7 pad_maximum_fusion.2.ta
  3.6 1.1 fusion.11
  4.7 0.8 pad_maximum_fusion.ub
  5.6 0.5 fusion.18
  6.1 0.7 pad_maximum_fusion.1.tb
  6.9 0.7 div.10.scaled
  7.6 0.0 copy-start
  7.6 11.6 %copy.41 = bf16[3072,16,128]{2,0,1:T(8,128)(2,1)} copy(bf16[3072,16,128]{2,1,0:T(8,128)(2,1)} %param.10) | data formatting | bytes 25165824 | tf_op args[4]
  19.1 0.0 copy-done
  19.2 1.5 copy.23
  20.6 0.0 copy-done.2
  20.6 0.6 reshape.609.qw
  21.2 199.6 %shard_map.64 = bf16[2,32,64,256]{3,2,1,0:T(8,128)(2,1)} custom-call(bf16[2,16,32,1024]{3,2,1,0:T(8,128)(2,1)} %bitcast.29, bf16[16,128,1024]{2,1,0:T(8,128)(2,1)} %leg.1, f32[4,256]{1,0:T(4,128)} %reshape.609.qw, s32[256]{0:T(256)} %orders.1, f32[2,48,512]{2,1,0:T(8,128)} %pad_maximum_fusion.2.ta, f32[2,64,512]{2,1,0:T(8,128)} %pad_maximum_fusion.1.tb, ...), custom_call_target="tpu_custom_call" | custom-call | flops 16999999488 | bytes 24000000 | tf_op jit(solution)/shard_map/pallas_call | solution.py:358
  220.9 0.0 copy-done.1
  220.9 0.5 copy.26
  221.4 2.3 %fusion.1 = bf16[256,8,2,256]{3,0,2,1:T(8,128)(2,1)S(1)} fusion(bf16[2,256,8,2,128]{4,2,3,1,0:T(8,128)(2,1)} %bitcast.31, bf16[8,2,16,8,256]{4,3,1,2,0:T(8,128)(2,1)S(1)} %bitcast.30), kind=kOutput, calls=%fused_computation.3 | convolution fusion | flops 537919488 | bytes 5242880 | tf_op jit(solution)/shard_map/jslcq,ljqr->slcr/dot_general | solution.py:396
  223.8 3.5 %copy.29 = bf16[256,8,2,256]{3,2,1,0:T(2,128)(2,1)} copy(bf16[256,8,2,256]{3,0,2,1:T(8,128)(2,1)S(1)} %fusion.1) | data formatting | bytes 4194304 | tf_op jit(solution)/shard_map/convert_element_type | solution.py:397
  (9 shorter events, 0.1 us)
Async XLA Ops:
  7.6 11.6 %copy-start = (bf16[16,1024,2,32]{1,3,2,0:T(8,128)(2,1)S(1)}, bf16[16,1024,2,32]{1,3,2,0:T(8,128)(2,1)}, u32[]{:S(2)}) copy-start(bf16[16,1024,2,32]{1,3,2,0:T(8,128)(2,1)} %param.6) | copy-start | bytes 6291460
  19.2 1.5 copy-start.2
  21.2 199.7 %copy-start.1 = (bf16[8,256,256]{2,1,0:T(8,128)(2,1)S(1)}, bf16[8,256,256]{2,1,0:T(8,128)(2,1)}, u32[]{:S(2)}) copy-start(bf16[8,256,256]{2,1,0:T(8,128)(2,1)} %param.11) | copy-start | bytes 3145732

commit v2 on v1

v2 whole, which is shorter than its diff:
```python
import math

import jax
import jax.numpy as jnp
from jax import lax
from jax.experimental import pallas as pl
from jax.experimental.pallas import tpu as pltpu
from jax.sharding import PartitionSpec as P

MESH = pl.DeviceIdType.MESH
F32, BF16 = jnp.float32, jnp.bfloat16
N_DEG = 1024
N_PHI = 3072
PEERS = 32
CHUNKS = 4
NT = (((1,), (1,)), ((), ()))
KB = 512
FB = 128


def wait_bytes(ref, sem):
    pltpu.make_async_copy(ref, ref, sem).wait()


def waves(product):
    turns = jnp.floor(product * (4.0 / N_PHI) + 0.5)
    x = (product - turns * (N_PHI // 4)) * (2.0 * math.pi / N_PHI)
    x2 = x * x
    sine = x * (1.0 + x2 * (-1 / 6 + x2 * (1 / 120 + x2 * (-1 / 5040 + x2 * (1 / 362880)))))
    cosine = 1.0 + x2 * (-0.5 + x2 * (1 / 24 + x2 * (-1 / 720 + x2 * (1 / 40320))))
    quarter = turns - 4.0 * jnp.floor(turns * 0.25)
    odd = (quarter == 1.0) | (quarter == 3.0)
    first = jnp.where(odd, sine, cosine)
    second = jnp.where(odd, cosine, sine)
    cos = jnp.where((quarter == 1.0) | (quarter == 2.0), -first, first)
    sin = jnp.where(quarter >= 2.0, -second, second)
    return cos, sin


def kernel(
    ent, leg, qw, orders, flow, out,
    ef, lg, wt, slope_t, fourier_t, fl, raw, tb, gsend, grecv, msend, mrecv, mx, wide, macc,
    r1send, r1recv, r2send, r2recv, fsend,
    ag_send, ag_recv, lg_send, lg_recv, raw_sem, g_send, g_recv, m_send, m_recv,
    r1_ssem, r1_rsem, r2_ssem, r2_rsem, f_send, f_recv,
):
    rad = lax.axis_index("rad")
    lat = lax.axis_index("lat")
    y, c = rad // 2, rad % 2
    me = 2 * lat + c
    up, down, across = (y + 1) % 4, (y + 3) % 4, (y + 2) % 4

    def place(index):
        return (2 * y + index % 2, index // 2)

    def raw_copy(block):
        rows = pl.ds(pl.multiple_of(FB * block, FB), FB)
        return pltpu.make_async_copy(flow.at[rows], raw.at[block % 2], raw_sem.at[block % 2])

    raw_copy(0).start()
    raw_copy(1).start()

    barrier = pltpu.get_barrier_semaphore()

    def greet(offset, carry):
        pl.semaphore_signal(
            barrier, inc=1, device_id=place((me + offset) % PEERS), device_id_type=MESH
        )
        return carry

    lax.fori_loop(1, PEERS, greet, 0)
    for row in (up, down):
        for core in range(2):
            pl.semaphore_signal(
                barrier, inc=1, device_id=(2 * row + core, lat), device_id_type=MESH
            )
    pl.semaphore_wait(barrier, PEERS - 1 + 4)

    def remote(src, dst, send_sem, recv_sem, device):
        pltpu.make_async_remote_copy(
            src_ref=src, dst_ref=dst, send_sem=send_sem, recv_sem=recv_sem,
            device_id=device, device_id_type=MESH,
        ).start()

    def all_to_all(source, target, send_sem, recv_sem):
        pltpu.make_async_copy(source(me), target, recv_sem).start()

        def send(offset, carry):
            dest = (me + offset) % PEERS
            remote(source(dest), target, send_sem, recv_sem, place(dest))
            return carry

        lax.fori_loop(1, PEERS, send, 0)

    def sent(buffer, sem):
        wait_bytes(buffer.at[pl.ds(0, PEERS - 1)], sem)

    def gather_direct(j):
        for row in (up, down):
            for core in range(2):
                remote(
                    ent.at[j, pl.ds(8 * core, 8)], ef.at[j, rad],
                    ag_send.at[j], ag_recv.at[j, rad], (2 * row + core, lat),
                )
        remote(
            ent.at[j, pl.ds(8 * (1 - c), 8)], ef.at[j, rad],
            ag_send.at[j], ag_recv.at[j, rad], (2 * y + 1 - c, lat),
        )
        pltpu.make_async_copy(ent.at[j, pl.ds(8 * c, 8)], ef.at[j, rad], ag_recv.at[j, rad]).start()

    def gather_wait(j, block):
        wait_bytes(ef.at[j, block], ag_recv.at[j, block])

    def gather_forward(j):
        for block, row in ((2 * down, up), (2 * up + 1, down)):
            gather_wait(j, block)
            remote(
                ef.at[j, block], ef.at[j, block],
                ag_send.at[j], ag_recv.at[j, block], (2 * row + c, lat),
            )

    def gather_rest(j):
        for block in (rad, 2 * y + 1 - c, 2 * down + 1, 2 * up, 2 * across, 2 * across + 1):
            gather_wait(j, block)

    columns = lax.broadcasted_iota(jnp.int32, (1, 512), 1)
    column_slots = (columns // 16) * 8 + columns % 8

    def column_order(slot, row):
        return jnp.where(column_slots == slot, orders[slot].astype(F32), row)

    def slope_rows(m_row):
        quarter = jnp.where(columns % 16 >= 8, N_PHI / 4, 0.0)
        cos_b, sin_b = waves(lax.broadcasted_iota(jnp.int32, (64, 512), 0).astype(F32) * m_row)
        tb[0] = cos_b
        tb[1] = sin_b
        scaled = m_row * (1.0 / N_DEG)

        def rows(a, carry):
            cos_a, sin_a = waves((64 * a).astype(F32) * m_row + quarter)
            sines = sin_a * tb[0] + cos_a * tb[1]
            slope_t[pl.ds(pl.multiple_of(64 * a, 64), 64), :] = (-(scaled * sines)).astype(BF16)
            return carry

        lax.fori_loop(0, N_PHI // 64, rows, 0)

    def fourier_rows(m_row):
        macc[:, :128] = jnp.transpose(jnp.broadcast_to(m_row, (128, 512)))
        lanes = lax.broadcasted_iota(jnp.int32, (64, 128), 1).astype(F32)
        second = lax.broadcasted_iota(jnp.int32, (64, 128), 0) % 16 >= 8
        quarter = jnp.where(second, N_PHI / 4, 0.0)

        def rows_of(block, carry):
            rows = pl.ds(pl.multiple_of(64 * block, 64), 64)
            m = macc[rows, :128]
            cos_b, sin_b = waves(lanes * m)
            cos_a, sin_a = waves(jnp.minimum(lanes, N_PHI // 128 - 1) * 128.0 * m + quarter)
            for a in range(N_PHI // 128):
                cosines = cos_a[:, a : a + 1] * cos_b - sin_a[:, a : a + 1] * sin_b
                fourier_t[rows, 128 * a : 128 * a + 128] = cosines.astype(BF16)
            return carry

        lax.fori_loop(0, 8, rows_of, 0)

    def turn_flow(block, carry):
        raw_copy(block).wait()
        piece = raw[block % 2].reshape(2, 64 * 16, 128)
        for half in range(2):
            wide[half] = piece[half].astype(F32)

        @pl.when(block + 2 < N_PHI // FB)
        def _():
            raw_copy(block + 2).start()

        for half in range(2):
            rows = pl.ds(pl.multiple_of(FB * block + 64 * half, 64), 64)
            for level in range(16):
                fl[level, rows, :] = wide[half, pl.ds(level, 64, stride=16), :].astype(BF16)
        return carry

    def tables(slot, carry):
        order = orders[16 * lat + 8 * c + slot]
        table = lg[slot]
        degrees = lax.broadcasted_iota(jnp.int32, table.shape, 1)
        lg[slot] = jnp.where(degrees >= order, table, jnp.zeros_like(table))
        turned = jnp.transpose(table.astype(F32))
        weights = jnp.concatenate([qw[pl.ds(2 * y, 1), :], qw[pl.ds(2 * y + 1, 1), :]], axis=1)
        weighted = turned * weights
        degrees = lax.broadcasted_iota(jnp.int32, turned.shape, 0)
        wt[slot] = jnp.where(degrees >= order, weighted, 0.0).astype(BF16)
        return carry

    def synthesize(j):
        gather_rest(j)

        def one(slot, carry):
            coeffs = ef[j, :, slot].reshape(128, N_DEG)
            values = lax.dot_general(coeffs, lg[slot], NT, preferred_element_type=F32)
            for block in range(8):
                for part in range(2):
                    at = 16 * block + 8 * part
                    for core in range(2):
                        wide[core, pl.ds(128 * block + 8 * part + slot, 8, stride=16), :] = values[
                            at : at + 8, 128 * core : 128 * core + 128
                        ]
            return carry

        lax.fori_loop(0, 8, one, 0)
        buf = j % 2
        if j >= 2:
            sent(gsend.at[buf], g_send.at[j - 2])

        def pack(p, carry):
            rows = pl.ds(pl.multiple_of(64 * p, 64), 64)
            for core in range(2):
                gsend[buf, 2 * p + core] = wide[core, rows, :].astype(BF16).reshape(4, 16, 128)
            return carry

        lax.fori_loop(0, 16, pack, 0)
        all_to_all(
            lambda dest: gsend.at[buf, dest], grecv.at[j, :, pl.ds(16 * me, 16), :],
            g_send.at[j], g_recv.at[j],
        )

    def grid(j):
        wait_bytes(grecv.at[j], g_recv.at[j])
        buf = j % 2
        if j >= 2:
            sent(msend.at[buf], m_send.at[j - 2])

        def pair(ip, carry):
            macc[...] = jnp.zeros_like(macc)

            def longitudes(kb, inner):
                rows = pl.ds(pl.multiple_of(KB * kb, KB), KB)
                points = jnp.concatenate([grecv[j, 2 * ip], grecv[j, 2 * ip + 1]], axis=1)
                slope = jnp.dot(slope_t[rows, :], points, preferred_element_type=F32)
                level = 4 * j + 2 * ip
                speed = jnp.concatenate([fl[level, rows, :], fl[level + 1, rows, :]], axis=1)
                forcing = (-speed.astype(F32) * slope).astype(BF16)
                macc[...] += jnp.dot(fourier_t[:, rows], forcing, preferred_element_type=F32)
                return inner

            lax.fori_loop(0, N_PHI // KB, longitudes, 0)
            done = (macc[...] * (2.0 / N_PHI)).astype(BF16)
            for half in range(2):
                msend[buf, :, 2 * ip + half] = done[:, 128 * half : 128 * half + 128].reshape(
                    PEERS, 16, 128
                )
            return carry

        lax.fori_loop(0, 2, pair, 0)
        all_to_all(
            lambda dest: msend.at[buf, dest], mrecv.at[j, me], m_send.at[j], m_recv.at[j]
        )

    def arrange(j):
        wait_bytes(mrecv.at[j], m_recv.at[j])

        def unpack(p, carry):
            rows = pl.ds(pl.multiple_of(64 * p, 64), 64)
            for core in range(2):
                wide[core, rows, :] = mrecv[j, 2 * p + core].reshape(64, 128).astype(F32)
            return carry

        lax.fori_loop(0, 16, unpack, 0)

        def one(slot, carry):
            for part in range(2):
                for block in range(0, 8, 2):
                    tiles = [
                        [
                            wide[core, pl.ds(128 * (block + q) + 8 * part + slot, 8, stride=16), :]
                            for core in range(2)
                        ]
                        for q in range(2)
                    ]
                    both = jnp.concatenate(
                        [jnp.concatenate(pieces, axis=1) for pieces in tiles], axis=0
                    )
                    at = 64 * part + 8 * block
                    mx[j, slot, at : at + 16, :] = both.astype(BF16)
            return carry

        lax.fori_loop(0, 8, one, 0)

    def partial(j, slot, quarter):
        rows = pl.ds(pl.multiple_of(256 * quarter, 256), 256)
        return lax.dot_general(wt[slot, rows, :], mx[j, slot], NT, preferred_element_type=F32)

    def reduce_first(j):
        buf = j % 2
        if j >= 2:
            wait_bytes(r1send.at[buf], r1_ssem.at[j - 2])
            wait_bytes(r2send.at[buf], r2_ssem.at[j - 2])

        def far(slot, carry):
            r1send[buf, slot] = partial(j, slot, across).astype(BF16)
            return carry

        for half, row in ((0, up), (1, down)):
            lax.fori_loop(4 * half, 4 * half + 4, far, 0)
            span = pl.ds(4 * half, 4)
            remote(
                r1send.at[buf, span], r1recv.at[j, span],
                r1_ssem.at[j], r1_rsem.at[j, half], (2 * row + c, lat),
            )
        for way, row, half in ((0, up, 1), (1, down, 0)):

            def near(slot, carry):
                r2send[buf, way, slot] = partial(j, slot, row).astype(BF16)
                return carry

            lax.fori_loop(4 * half, 4 * half + 4, near, 0)
            reduce_send(j, way, row, half)

    def reduce_send(j, way, row, half):
        span = pl.ds(4 * half, 4)
        remote(
            r2send.at[j % 2, way, span], r2recv.at[j, way, span],
            r2_ssem.at[j], r2_rsem.at[j, way, half], (2 * row + c, lat),
        )

    def reduce_second(j):
        for way, row, half in ((0, up, 0), (1, down, 1)):
            span = pl.ds(4 * half, 4)
            wait_bytes(r1recv.at[j, span], r1_rsem.at[j, half])

            def near(slot, carry):
                total = partial(j, slot, row) + r1recv[j, slot].astype(F32)
                r2send[j % 2, way, slot] = total.astype(BF16)
                return carry

            lax.fori_loop(4 * half, 4 * half + 4, near, 0)
            reduce_send(j, way, row, half)

    def finish(j):
        buf = j % 2
        for way in range(2):
            for half in range(2):
                span = pl.ds(4 * half, 4)
                wait_bytes(r2recv.at[j, way, span], r2_rsem.at[j, way, half])
        lanes = pl.ds(pl.multiple_of(256 * y, 256), 256)
        eye = (
            lax.broadcasted_iota(jnp.int32, (256, 256), 0)
            == lax.broadcasted_iota(jnp.int32, (256, 256), 1)
        ).astype(F32).astype(BF16)

        def one(slot, carry):
            own = ef[j, :, slot, :, lanes].astype(F32)
            own = jnp.concatenate([own[:, :8], own[:, 8:]], axis=0).reshape(128, 256)
            total = partial(j, slot, y) + lax.dot_general(
                eye, own.astype(BF16), NT, preferred_element_type=F32
            )
            total += r2recv[j, 0, slot].astype(F32) + r2recv[j, 1, slot].astype(F32)
            for core in range(2):
                for p in range(16):
                    at = 128 * core + 8 * p
                    wide[core, pl.ds(64 * p + slot, 8, stride=8), :] = total[at : at + 8]
            return carry

        lax.fori_loop(0, 8, one, 0)
        if j >= 2:
            sent(fsend.at[buf], f_send.at[j - 2])
            wait_bytes(out.at[j - 2], f_recv.at[j - 2])

        def pack(p, carry):
            rows = pl.ds(pl.multiple_of(64 * p, 64), 64)
            for core in range(2):
                fsend[buf, 2 * p + core] = wide[core, rows, :].astype(BF16)
            return carry

        lax.fori_loop(0, 16, pack, 0)
        all_to_all(lambda dest: fsend.at[buf, dest], out.at[j, me], f_send.at[j], f_recv.at[j])

    gather_direct(0)
    mine = pl.ds(pl.multiple_of(128 * c, 128), 128)
    remote(
        leg.at[pl.ds(8 * (1 - c), 8)], lg.at[:, mine, :], lg_send, lg_recv, (2 * y + 1 - c, lat)
    )
    pltpu.make_async_copy(leg.at[pl.ds(8 * c, 8)], lg.at[:, mine, :], lg_recv).start()
    m_row = lax.fori_loop(0, 256, column_order, jnp.zeros((1, 512), F32))
    slope_rows(m_row)
    fourier_rows(m_row)
    lax.fori_loop(0, 12, turn_flow, 0)
    gather_forward(0)
    gather_direct(1)
    gather_direct(2)
    lax.fori_loop(12, N_PHI // FB, turn_flow, 0)
    wait_bytes(lg, lg_recv)
    lax.fori_loop(0, 8, tables, 0)
    synthesize(0)
    gather_forward(1)
    gather_direct(3)
    grid(0)
    synthesize(1)
    gather_forward(2)
    arrange(0)
    reduce_first(0)
    grid(1)
    synthesize(2)
    gather_forward(3)
    reduce_second(0)
    arrange(1)
    reduce_first(1)
    grid(2)
    synthesize(3)
    finish(0)
    reduce_second(1)
    arrange(2)
    reduce_first(2)
    grid(3)
    finish(1)
    reduce_second(2)
    arrange(3)
    reduce_first(3)
    finish(2)
    reduce_second(3)
    finish(3)
    for j in range(CHUNKS):
        wait_bytes(ef.at[j, pl.ds(0, 7)], ag_send.at[j])
    for j in range(CHUNKS - 2, CHUNKS):
        sent(gsend.at[j % 2], g_send.at[j])
        sent(msend.at[j % 2], m_send.at[j])
        wait_bytes(r1send.at[j % 2], r1_ssem.at[j])
        wait_bytes(r2send.at[j % 2], r2_ssem.at[j])
        sent(fsend.at[j % 2], f_send.at[j])
        wait_bytes(out.at[j], f_recv.at[j])
    wait_bytes(lg.at[:, pl.ds(0, 128), :], lg_send)


def radial_kernel(sides, inverses, out):
    source = lax.broadcasted_iota(jnp.int32, (256, 512), 0)
    lane = lax.broadcasted_iota(jnp.int32, (256, 512), 1)
    chunk, rest = lane // 128, lane % 128
    level = (rest % 64) // 4 * 16 + chunk * 4 + rest % 4
    hits = (source == level).astype(F32)
    part = rest // 64

    def two_degrees(index, carry):
        rows = pl.ds(pl.multiple_of(16 * index, 16), 16)
        piece = sides[:, :, rows, :].astype(F32)
        for u in range(2):
            flat = piece[:, :, 8 * u : 8 * u + 8, :].reshape(CHUNKS, 256, 128).astype(BF16)
            left = jnp.concatenate([flat[j] for j in range(CHUNKS)], axis=1)
            inverse = inverses[2 * index + u]
            for half in range(2):
                spread = jnp.where(part == half, hits, 0.0).astype(BF16)
                right = jnp.dot(inverse, spread, preferred_element_type=F32).astype(BF16)
                out[2 * index + u, :, 256 * half : 256 * half + 256] = lax.dot_general(
                    left, right, NT, preferred_element_type=F32
                ).astype(BF16)
        return carry

    lax.fori_loop(0, 4, two_degrees, 0)


def shards(entropy, legendre, quad_weights, azimuthal_orders, azimuthal_flow, radial_inverses):
    ent = jnp.transpose(entropy, (0, 2, 3, 1)).reshape(16, 2, 2, CHUNKS, 4, N_DEG)
    ent = jnp.transpose(ent, (3, 0, 1, 2, 4, 5)).reshape(CHUNKS, 16, 16, N_DEG)
    hbm = pl.BlockSpec(memory_space=pl.ANY)
    vmem = pl.BlockSpec(memory_space=pltpu.VMEM)
    smem = pl.BlockSpec(memory_space=pltpu.SMEM)
    dma = pltpu.SemaphoreType.DMA
    received = pl.pallas_call(
        kernel,
        out_shape=jax.ShapeDtypeStruct((CHUNKS, PEERS, 64, 128), BF16),
        in_specs=[hbm, hbm, vmem, smem, hbm],
        out_specs=hbm,
        scratch_shapes=[
            pltpu.VMEM((CHUNKS, 8, 8, 16, N_DEG), BF16),
            pltpu.VMEM((8, 256, N_DEG), BF16),
            pltpu.VMEM((8, N_DEG, 256), BF16),
            pltpu.VMEM((N_PHI, 512), BF16),
            pltpu.VMEM((512, N_PHI), BF16),
            pltpu.VMEM((16, N_PHI, 128), BF16),
            pltpu.VMEM((2, FB, 16, 128), BF16),
            pltpu.VMEM((2, 64, 512), F32),
            pltpu.VMEM((2, PEERS, 4, 16, 128), BF16),
            pltpu.VMEM((CHUNKS, 4, 512, 128), BF16),
            pltpu.VMEM((2, PEERS, 4, 16, 128), BF16),
            pltpu.VMEM((CHUNKS, PEERS, 4, 16, 128), BF16),
            pltpu.VMEM((CHUNKS, 8, 128, 256), BF16),
            pltpu.VMEM((2, 1024, 128), F32),
            pltpu.VMEM((512, 256), F32),
            pltpu.VMEM((2, 8, 256, 128), BF16),
            pltpu.VMEM((CHUNKS, 8, 256, 128), BF16),
            pltpu.VMEM((2, 2, 8, 256, 128), BF16),
            pltpu.VMEM((CHUNKS, 2, 8, 256, 128), BF16),
            pltpu.VMEM((2, PEERS, 64, 128), BF16),
            dma((CHUNKS,)), dma((CHUNKS, 8)), dma, dma, dma((2,)),
            dma((CHUNKS,)), dma((CHUNKS,)), dma((CHUNKS,)), dma((CHUNKS,)),
            dma((CHUNKS,)), dma((CHUNKS, 2)), dma((CHUNKS,)), dma((CHUNKS, 2, 2)),
            dma((CHUNKS,)), dma((CHUNKS,)),
        ],
        compiler_params=pltpu.CompilerParams(
            collective_id=0, has_side_effects=True, vmem_limit_bytes=62 * 1024 * 1024
        ),
        cost_estimate=pl.CostEstimate(
            flops=17_000_000_000, bytes_accessed=24_000_000, transcendentals=0
        ),
    )(ent, legendre, quad_weights.reshape(8, 128), azimuthal_orders, azimuthal_flow)
    updated = pl.pallas_call(
        radial_kernel,
        out_shape=jax.ShapeDtypeStruct((8, 256, 512), BF16),
        in_specs=[vmem, vmem],
        out_specs=vmem,
        compiler_params=pltpu.CompilerParams(vmem_limit_bytes=32 * 1024 * 1024),
        cost_estimate=pl.CostEstimate(
            flops=3_200_000_000, bytes_accessed=6_000_000, transcendentals=0
        ),
    )(received, radial_inverses)
    return jnp.transpose(updated.reshape(8, 256, 2, 256), (1, 0, 2, 3))


def solution(mesh):
    placed = (
        P("lat", None, None, "rad"),
        P("lat", "rad", None),
        P(),
        P(),
        P(None, "lat", "rad"),
        P(("rad", "lat"), None, None),
    )
    return jax.shard_map(
        shards,
        mesh=mesh,
        in_specs=placed,
        out_specs=P(None, ("rad", "lat"), None, None),
        check_vma=False,
    )
```

time: 227 us -> 197 us (0.87)
  Pallas kernels: 200 us -> 179 us
  other arithmetic: 4.72 us -> 0 us
  local copies, waits for them, and re-layouts: 20.5 us -> 17 us
  matrix products: 2.32 us -> 0 us
    pallas_call x1 -> x2, Pallas kernels: 200 us -> 179 us  [the longest x1 175 us: shards(): pl.pallas_call(kernel, out_shape=jax.ShapeDtypeStruct((CHUNKS, PEERS, 64,...]
    reshape x2 -> x5, local copies, waits for them, and re-layouts: 2.09 us -> 15.4 us  [the longest x2 6.96 us: shards(): jnp.transpose(entropy, (0, 2, 3, 1)).reshape(16, 2, 2, CHUNKS, 4, N_DEG)]
    unnamed x8 -> x4, local copies, waits for them, and re-layouts: 12.1 us -> 1.59 us
    convert_element_type x1 -> x0, local copies, waits for them, and re-layouts: 3.48 us -> none  [shards(): return updated.astype(BF16)]
    cos x4 -> x0, other arithmetic: 2.44 us -> none  [waves(): return jnp.stack([jnp.cos(angles), jnp.sin(angles)])]
    dot_general x1 -> x0, matrix products: 2.32 us -> none  [shards(): jnp.einsum('jslcq,ljqr->slcr', sides, inverses, preferred_element_type=F32)]
where the time goes in v2:
time: 197 us; the launch traced here: 196 us
  Pallas kernels  179 us (91%)
  local copies, waits for them, and re-layouts  17 us (9%)
    pallas_call x1, Pallas kernels, shards(): pl.pallas_call(kernel, out_shape=jax.ShapeDtypeStruct((CHUNKS, PEERS, 64,...  175 us
    reshape x2, local copies, waits for them, and re-layouts, shards(): jnp.transpose(entropy, (0, 2, 3, 1)).reshape(16, 2, 2, CHUNKS, 4, N_DEG)  6.96 us
    reshape x2, local copies, waits for them, and re-layouts, shards(): return jnp.transpose(updated.reshape(8, 256, 2, 256), (1, 0, 2, 3))  6.42 us
    pallas_call x1, Pallas kernels, shards(): pl.pallas_call(radial_kernel, out_shape=jax.ShapeDtypeStruct((8, 256, 512...  4.26 us

profile of v2, /device:TPU:1, one launch (start us, length us, event | category | flops | bytes accessed | tf_op | source)
XLA Modules:
  0.0 196.1 jit_solution(15070335419200936442)
XLA Ops:
  0.0 4.1 %reshape.12 = bf16[16,2,2,4,4,1024]{5,4,3,2,1,0:T(4,128)(2,1)} reshape(bf16[16,2,32,1024]{3,2,1,0:T(8,128)(2,1)} %bitcast.11) | data formatting | bytes 4194304 | tf_op jit(solution)/shard_map/reshape | solution.py:459
  4.1 2.9 %copy.12 = bf16[16,2,2,4,4,1024]{5,4,2,1,0,3:T(4,128)(2,1)S(1)} copy(bf16[16,2,2,4,4,1024]{5,4,3,2,1,0:T(4,128)(2,1)} %reshape.12) | data formatting | bytes 4194304 | tf_op jit(solution)/shard_map/reshape | solution.py:459
  7.0 2.0 %reshape.13.ent = bf16[4,16,16,1024]{3,2,1,0:T(8,128)(2,1)} reshape(bf16[4,16,2,2,4,1024]{5,4,3,2,1,0:T(4,128)(2,1)S(1)} %bitcast.10) | data formatting | bytes 4194304 | tf_op jit(solution)/shard_map/reshape | solution.py:460
  9.0 0.0 copy-start
  9.0 174.8 %shard_map.64.sides = bf16[4,32,64,128]{3,2,1,0:T(8,128)(2,1)} custom-call(bf16[4,16,16,1024]{3,2,1,0:T(8,128)(2,1)} %reshape.13.ent, bf16[16,128,1024]{2,1,0:T(8,128)(2,1)} %leg.1, f32[8,128]{1,0:T(8,128)} %bitcast.12, s32[256]{0:T(256)} %orders.1, bf16[3072,16,128]{2,1,0:T(8,128)(2,1)} %flow.1), custom_call_target="tpu_custom_call" | custom-call | flops 16999999488 | bytes 24000000 | tf_op jit(solution)/shard_map/pallas_call | solution.py:465
  183.8 0.0 copy-done
  183.8 0.0 copy-start.1
  183.8 1.6 copy-done.1
  185.4 4.3 %shard_map.65 = bf16[8,256,512]{2,1,0:T(8,128)(2,1)S(1)} custom-call(bf16[4,32,64,128]{3,2,1,0:T(8,128)(2,1)S(1)} %copy-done.1, bf16[8,256,256]{2,1,0:T(8,128)(2,1)S(1)} %copy-done), custom_call_target="tpu_custom_call" | custom-call | flops 3200000000 | bytes 6000000 | tf_op jit(solution)/shard_map/pallas_call | solution.py:503
  189.7 2.1 %reshape.15 = bf16[8,256,2,256]{3,2,1,0:T(2,128)(2,1)} reshape(bf16[8,256,512]{2,1,0:T(8,128)(2,1)S(1)} %shard_map.65) | data formatting | bytes 4194304 | tf_op jit(solution)/shard_map/reshape | solution.py:513
  191.8 4.3 %copy.11 = bf16[8,256,2,256]{3,2,0,1:T(2,128)(2,1)} copy(bf16[8,256,2,256]{3,2,1,0:T(2,128)(2,1)} %reshape.15) | data formatting | bytes 4194304 | tf_op jit(solution)/shard_map/reshape | solution.py:513
Async XLA Ops:
  9.0 174.8 %copy-start = (bf16[8,256,256]{2,1,0:T(8,128)(2,1)S(1)}, bf16[8,256,256]{2,1,0:T(8,128)(2,1)}, u32[]{:S(2)}) copy-start(bf16[8,256,256]{2,1,0:T(8,128)(2,1)} %inverses.1) | copy-start | bytes 3145732
  183.8 1.6 copy-start.1

commit v3 on v2

--- a/solution.py
+++ b/solution.py
@@ -14,8 +14,8 @@
 PEERS = 32
 CHUNKS = 4
 NT = (((1,), (1,)), ((), ()))
-KB = 512
-FB = 128
+KB = 256
+FB = 64
 
 
 def wait_bytes(ref, sem):
@@ -38,11 +38,11 @@
 
 
 def kernel(
-    ent, leg, qw, orders, flow, out,
-    ef, lg, wt, slope_t, fourier_t, fl, raw, tb, gsend, grecv, msend, mrecv, mx, wide, macc,
+    ent, leg, qw, orders, flow, inverses, out,
+    er, inv, fr, ef, lg, wt, slope_t, fourier_t, fl, raw, tb, gsend, grecv, msend, mrecv, mx, wide, macc,
     r1send, r1recv, r2send, r2recv, fsend,
     ag_send, ag_recv, lg_send, lg_recv, raw_sem, g_send, g_recv, m_send, m_recv,
-    r1_ssem, r1_rsem, r2_ssem, r2_rsem, f_send, f_recv,
+    r1_ssem, r1_rsem, r2_ssem, r2_rsem, f_send, f_recv, er_sem, inv_sem, out_sem,
 ):
     rad = lax.axis_index("rad")
     lat = lax.axis_index("lat")
@@ -57,8 +57,12 @@
         rows = pl.ds(pl.multiple_of(FB * block, FB), FB)
         return pltpu.make_async_copy(flow.at[rows], raw.at[block % 2], raw_sem.at[block % 2])
 
+    own_rows = pltpu.make_async_copy(ent, er, er_sem)
+    own_rows.start()
     raw_copy(0).start()
     raw_copy(1).start()
+    own_inverses = pltpu.make_async_copy(inverses, inv, inv_sem)
+    own_inverses.start()
 
     barrier = pltpu.get_barrier_semaphore()
 
@@ -74,6 +78,24 @@
             pl.semaphore_signal(
                 barrier, inc=1, device_id=(2 * row + core, lat), device_id_type=MESH
             )
+
+    def regroup(slot, carry):
+        rows = er[slot].astype(F32).reshape(4, 16, N_DEG)
+        low = lax.broadcasted_iota(jnp.int32, (8, N_DEG), 0) < 4
+        for j in range(CHUNKS):
+            tiles = []
+            for part in range(2):
+                first = rows[2 * part, 8 * (j // 2) : 8 * (j // 2) + 8]
+                second = rows[2 * part + 1, 8 * (j // 2) : 8 * (j // 2) + 8]
+                if j % 2 == 0:
+                    tiles.append(jnp.where(low, first, pltpu.roll(second, 4, axis=0)))
+                else:
+                    tiles.append(jnp.where(low, pltpu.roll(first, 4, axis=0), second))
+            er[slot, 16 * j : 16 * j + 16, :] = jnp.concatenate(tiles, axis=0).astype(BF16)
+        return carry
+
+    own_rows.wait()
+    lax.fori_loop(0, 16, regroup, 0)
     pl.semaphore_wait(barrier, PEERS - 1 + 4)
 
     def remote(src, dst, send_sem, recv_sem, device):
@@ -96,17 +118,20 @@
         wait_bytes(buffer.at[pl.ds(0, PEERS - 1)], sem)
 
     def gather_direct(j):
+        rows = pl.ds(16 * j, 16)
         for row in (up, down):
             for core in range(2):
                 remote(
-                    ent.at[j, pl.ds(8 * core, 8)], ef.at[j, rad],
+                    er.at[pl.ds(8 * core, 8), rows, :], ef.at[j, rad],
                     ag_send.at[j], ag_recv.at[j, rad], (2 * row + core, lat),
                 )
         remote(
-            ent.at[j, pl.ds(8 * (1 - c), 8)], ef.at[j, rad],
+            er.at[pl.ds(8 * (1 - c), 8), rows, :], ef.at[j, rad],
             ag_send.at[j], ag_recv.at[j, rad], (2 * y + 1 - c, lat),
         )
-        pltpu.make_async_copy(ent.at[j, pl.ds(8 * c, 8)], ef.at[j, rad], ag_recv.at[j, rad]).start()
+        pltpu.make_async_copy(
+            er.at[pl.ds(8 * c, 8), rows, :], ef.at[j, rad], ag_recv.at[j, rad]
+        ).start()
 
     def gather_wait(j, block):
         wait_bytes(ef.at[j, block], ag_recv.at[j, block])
@@ -164,30 +189,33 @@
 
     def turn_flow(block, carry):
         raw_copy(block).wait()
-        piece = raw[block % 2].reshape(2, 64 * 16, 128)
+        piece = raw[block % 2].reshape(2, FB * 8, 128)
         for half in range(2):
-            wide[half] = piece[half].astype(F32)
+            wide[half, : FB * 8, :] = piece[half].astype(F32)
 
         @pl.when(block + 2 < N_PHI // FB)
         def _():
             raw_copy(block + 2).start()
 
         for half in range(2):
-            rows = pl.ds(pl.multiple_of(FB * block + 64 * half, 64), 64)
+            rows = pl.ds(pl.multiple_of(FB * block + FB // 2 * half, FB // 2), FB // 2)
             for level in range(16):
-                fl[level, rows, :] = wide[half, pl.ds(level, 64, stride=16), :].astype(BF16)
-        return carry
-
-    def tables(slot, carry):
+                fl[level, rows, :] = wide[half, pl.ds(level, FB // 2, stride=16), :].astype(BF16)
+        return carry
+
+    def mask(slot, carry):
         order = orders[16 * lat + 8 * c + slot]
         table = lg[slot]
         degrees = lax.broadcasted_iota(jnp.int32, table.shape, 1)
         lg[slot] = jnp.where(degrees >= order, table, jnp.zeros_like(table))
-        turned = jnp.transpose(table.astype(F32))
+        return carry
+
+    def weigh(slot, carry):
         weights = jnp.concatenate([qw[pl.ds(2 * y, 1), :], qw[pl.ds(2 * y + 1, 1), :]], axis=1)
-        weighted = turned * weights
-        degrees = lax.broadcasted_iota(jnp.int32, turned.shape, 0)
-        wt[slot] = jnp.where(degrees >= order, weighted, 0.0).astype(BF16)
+        weighted = (jnp.transpose(lg[slot].astype(F32)) * weights).astype(BF16)
+        for quarter in range(4):
+            rows = pl.ds(pl.multiple_of(256 * ((quarter - y + 4) % 4), 256), 256)
+            wt[slot, rows, :] = weighted[256 * quarter : 256 * quarter + 256]
         return carry
 
     def synthesize(j):
@@ -228,28 +256,21 @@
         if j >= 2:
             sent(msend.at[buf], m_send.at[j - 2])
 
-        def pair(ip, carry):
-            macc[...] = jnp.zeros_like(macc)
-
-            def longitudes(kb, inner):
-                rows = pl.ds(pl.multiple_of(KB * kb, KB), KB)
-                points = jnp.concatenate([grecv[j, 2 * ip], grecv[j, 2 * ip + 1]], axis=1)
-                slope = jnp.dot(slope_t[rows, :], points, preferred_element_type=F32)
-                level = 4 * j + 2 * ip
-                speed = jnp.concatenate([fl[level, rows, :], fl[level + 1, rows, :]], axis=1)
-                forcing = (-speed.astype(F32) * slope).astype(BF16)
-                macc[...] += jnp.dot(fourier_t[:, rows], forcing, preferred_element_type=F32)
-                return inner
-
-            lax.fori_loop(0, N_PHI // KB, longitudes, 0)
-            done = (macc[...] * (2.0 / N_PHI)).astype(BF16)
-            for half in range(2):
-                msend[buf, :, 2 * ip + half] = done[:, 128 * half : 128 * half + 128].reshape(
-                    PEERS, 16, 128
-                )
-            return carry
-
-        lax.fori_loop(0, 2, pair, 0)
+        macc[...] = jnp.zeros_like(macc)
+
+        def longitudes(kb, carry):
+            rows = pl.ds(pl.multiple_of(KB * kb, KB), KB)
+            points = jnp.concatenate([grecv[j, i] for i in range(4)], axis=1)
+            slope = jnp.dot(slope_t[rows, :], points, preferred_element_type=F32)
+            speed = jnp.concatenate([fl[4 * j + i, rows, :] for i in range(4)], axis=1)
+            forcing = (-speed.astype(F32) * slope).astype(BF16)
+            macc[...] += jnp.dot(fourier_t[:, rows], forcing, preferred_element_type=F32)
+            return carry
+
+        lax.fori_loop(0, N_PHI // KB, longitudes, 0)
+        for i in range(4):
+            done = (macc[:, 128 * i : 128 * i + 128] * (2.0 / N_PHI)).astype(BF16)
+            msend[buf, :, i] = done.reshape(PEERS, 16, 128)
         all_to_all(
             lambda dest: msend.at[buf, dest], mrecv.at[j, me], m_send.at[j], m_recv.at[j]
         )
@@ -284,35 +305,30 @@
 
         lax.fori_loop(0, 8, one, 0)
 
-    def partial(j, slot, quarter):
-        rows = pl.ds(pl.multiple_of(256 * quarter, 256), 256)
-        return lax.dot_general(wt[slot, rows, :], mx[j, slot], NT, preferred_element_type=F32)
-
     def reduce_first(j):
         buf = j % 2
         if j >= 2:
             wait_bytes(r1send.at[buf], r1_ssem.at[j - 2])
             wait_bytes(r2send.at[buf], r2_ssem.at[j - 2])
 
-        def far(slot, carry):
-            r1send[buf, slot] = partial(j, slot, across).astype(BF16)
-            return carry
-
+        def foreign(slot, carry):
+            sums = lax.dot_general(
+                wt[slot, 256:, :], mx[j, slot], NT, preferred_element_type=F32
+            ).astype(BF16)
+            r2send[buf, 0, slot] = sums[:256]
+            r1send[buf, slot] = sums[256:512]
+            r2send[buf, 1, slot] = sums[512:]
+            return carry
+
+        lax.fori_loop(0, 8, foreign, 0)
         for half, row in ((0, up), (1, down)):
-            lax.fori_loop(4 * half, 4 * half + 4, far, 0)
             span = pl.ds(4 * half, 4)
             remote(
                 r1send.at[buf, span], r1recv.at[j, span],
                 r1_ssem.at[j], r1_rsem.at[j, half], (2 * row + c, lat),
             )
-        for way, row, half in ((0, up, 1), (1, down, 0)):
-
-            def near(slot, carry):
-                r2send[buf, way, slot] = partial(j, slot, row).astype(BF16)
-                return carry
-
-            lax.fori_loop(4 * half, 4 * half + 4, near, 0)
-            reduce_send(j, way, row, half)
+        reduce_send(j, 0, up, 1)
+        reduce_send(j, 1, down, 0)
 
     def reduce_send(j, way, row, half):
         span = pl.ds(4 * half, 4)
@@ -327,7 +343,7 @@
             wait_bytes(r1recv.at[j, span], r1_rsem.at[j, half])
 
             def near(slot, carry):
-                total = partial(j, slot, row) + r1recv[j, slot].astype(F32)
+                total = r2send[j % 2, way, slot].astype(F32) + r1recv[j, slot].astype(F32)
                 r2send[j % 2, way, slot] = total.astype(BF16)
                 return carry
 
@@ -349,9 +365,9 @@
         def one(slot, carry):
             own = ef[j, :, slot, :, lanes].astype(F32)
             own = jnp.concatenate([own[:, :8], own[:, 8:]], axis=0).reshape(128, 256)
-            total = partial(j, slot, y) + lax.dot_general(
-                eye, own.astype(BF16), NT, preferred_element_type=F32
-            )
+            total = lax.dot_general(
+                wt[slot, :256, :], mx[j, slot], NT, preferred_element_type=F32
+            ) + lax.dot_general(eye, own.astype(BF16), NT, preferred_element_type=F32)
             total += r2recv[j, 0, slot].astype(F32) + r2recv[j, 1, slot].astype(F32)
             for core in range(2):
                 for p in range(16):
@@ -362,7 +378,7 @@
         lax.fori_loop(0, 8, one, 0)
         if j >= 2:
             sent(fsend.at[buf], f_send.at[j - 2])
-            wait_bytes(out.at[j - 2], f_recv.at[j - 2])
+            wait_bytes(fr.at[j - 2], f_recv.at[j - 2])
 
         def pack(p, carry):
             rows = pl.ds(pl.multiple_of(64 * p, 64), 64)
@@ -371,7 +387,7 @@
             return carry
 
         lax.fori_loop(0, 16, pack, 0)
-        all_to_all(lambda dest: fsend.at[buf, dest], out.at[j, me], f_send.at[j], f_recv.at[j])
+        all_to_all(lambda dest: fsend.at[buf, dest], fr.at[j, me], f_send.at[j], f_recv.at[j])
 
     gather_direct(0)
     mine = pl.ds(pl.multiple_of(128 * c, 128), 128)
@@ -379,37 +395,66 @@
         leg.at[pl.ds(8 * (1 - c), 8)], lg.at[:, mine, :], lg_send, lg_recv, (2 * y + 1 - c, lat)
     )
     pltpu.make_async_copy(leg.at[pl.ds(8 * c, 8)], lg.at[:, mine, :], lg_recv).start()
+    def spread(degree, carry):
+        source = lax.broadcasted_iota(jnp.int32, (256, 512), 0)
+        lane = lax.broadcasted_iota(jnp.int32, (256, 512), 1)
+        level = (lane % 64) // 4 * 16 + lane // 128 * 4 + lane % 4
+        hits = (source == level).astype(F32).astype(BF16)
+        lg[degree, :, :512] = jnp.dot(inv[degree], hits, preferred_element_type=F32).astype(BF16)
+        return carry
+
+    def out_copy(degree):
+        return pltpu.make_async_copy(wt.at[degree, pl.ds(0, 512), :], out.at[degree], out_sem)
+
+    def radial(index, carry):
+        rows = pl.ds(pl.multiple_of(16 * index, 16), 16)
+        part = lax.broadcasted_iota(jnp.int32, (256, 512), 1) % 128 // 64
+        piece = fr[:, :, rows, :].astype(F32)
+        for u in range(2):
+            flat = piece[:, :, 8 * u : 8 * u + 8, :].reshape(CHUNKS, 256, 128)
+            left = jnp.concatenate([flat[j] for j in range(CHUNKS)], axis=1)
+            degree = 2 * index + u
+            for half in range(2):
+                wt[degree, 256 * half : 256 * half + 256, :] = lax.dot_general(
+                    jnp.where(part == half, left, 0.0).astype(BF16), lg[degree, :, :512], NT,
+                    preferred_element_type=F32,
+                ).astype(BF16)
+            out_copy(degree).start()
+        return carry
+
+    gather_direct(1)
+    wait_bytes(lg, lg_recv)
+    lax.fori_loop(0, 8, mask, 0)
+    lax.fori_loop(0, 8, weigh, 0)
+    gather_forward(0)
+    lax.fori_loop(0, N_PHI // FB, turn_flow, 0)
+    gather_forward(1)
     m_row = lax.fori_loop(0, 256, column_order, jnp.zeros((1, 512), F32))
     slope_rows(m_row)
     fourier_rows(m_row)
-    lax.fori_loop(0, 12, turn_flow, 0)
-    gather_forward(0)
-    gather_direct(1)
+    synthesize(0)
     gather_direct(2)
-    lax.fori_loop(12, N_PHI // FB, turn_flow, 0)
-    wait_bytes(lg, lg_recv)
-    lax.fori_loop(0, 8, tables, 0)
-    synthesize(0)
-    gather_forward(1)
     gather_direct(3)
+    synthesize(1)
     grid(0)
-    synthesize(1)
     gather_forward(2)
+    grid(1)
+    gather_forward(3)
     arrange(0)
     reduce_first(0)
-    grid(1)
     synthesize(2)
-    gather_forward(3)
-    reduce_second(0)
+    synthesize(3)
     arrange(1)
     reduce_first(1)
+    reduce_second(0)
     grid(2)
-    synthesize(3)
-    finish(0)
     reduce_second(1)
+    grid(3)
+    own_inverses.wait()
+    lax.fori_loop(0, 8, spread, 0)
     arrange(2)
     reduce_first(2)
-    grid(3)
+    finish(0)
     finish(1)
     reduce_second(2)
     arrange(3)
@@ -425,49 +470,27 @@
         wait_bytes(r1send.at[j % 2], r1_ssem.at[j])
         wait_bytes(r2send.at[j % 2], r2_ssem.at[j])
         sent(fsend.at[j % 2], f_send.at[j])
-        wait_bytes(out.at[j], f_recv.at[j])
+        wait_bytes(fr.at[j], f_recv.at[j])
     wait_bytes(lg.at[:, pl.ds(0, 128), :], lg_send)
-
-
-def radial_kernel(sides, inverses, out):
-    source = lax.broadcasted_iota(jnp.int32, (256, 512), 0)
-    lane = lax.broadcasted_iota(jnp.int32, (256, 512), 1)
-    chunk, rest = lane // 128, lane % 128
-    level = (rest % 64) // 4 * 16 + chunk * 4 + rest % 4
-    hits = (source == level).astype(F32)
-    part = rest // 64
-
-    def two_degrees(index, carry):
-        rows = pl.ds(pl.multiple_of(16 * index, 16), 16)
-        piece = sides[:, :, rows, :].astype(F32)
-        for u in range(2):
-            flat = piece[:, :, 8 * u : 8 * u + 8, :].reshape(CHUNKS, 256, 128).astype(BF16)
-            left = jnp.concatenate([flat[j] for j in range(CHUNKS)], axis=1)
-            inverse = inverses[2 * index + u]
-            for half in range(2):
-                spread = jnp.where(part == half, hits, 0.0).astype(BF16)
-                right = jnp.dot(inverse, spread, preferred_element_type=F32).astype(BF16)
-                out[2 * index + u, :, 256 * half : 256 * half + 256] = lax.dot_general(
-                    left, right, NT, preferred_element_type=F32
-                ).astype(BF16)
-        return carry
-
-    lax.fori_loop(0, 4, two_degrees, 0)
+    lax.fori_loop(0, 4, radial, 0)
+    wait_bytes(wt.at[:, pl.ds(0, 512), :], out_sem)
 
 
 def shards(entropy, legendre, quad_weights, azimuthal_orders, azimuthal_flow, radial_inverses):
-    ent = jnp.transpose(entropy, (0, 2, 3, 1)).reshape(16, 2, 2, CHUNKS, 4, N_DEG)
-    ent = jnp.transpose(ent, (3, 0, 1, 2, 4, 5)).reshape(CHUNKS, 16, 16, N_DEG)
+    ent = jnp.transpose(entropy, (0, 2, 3, 1)).reshape(16, 64, N_DEG)
     hbm = pl.BlockSpec(memory_space=pl.ANY)
     vmem = pl.BlockSpec(memory_space=pltpu.VMEM)
     smem = pl.BlockSpec(memory_space=pltpu.SMEM)
     dma = pltpu.SemaphoreType.DMA
-    received = pl.pallas_call(
+    updated = pl.pallas_call(
         kernel,
-        out_shape=jax.ShapeDtypeStruct((CHUNKS, PEERS, 64, 128), BF16),
-        in_specs=[hbm, hbm, vmem, smem, hbm],
+        out_shape=jax.ShapeDtypeStruct((8, 512, 256), BF16),
+        in_specs=[hbm, hbm, vmem, smem, hbm, hbm],
         out_specs=hbm,
         scratch_shapes=[
+            pltpu.VMEM((16, 64, N_DEG), BF16),
+            pltpu.VMEM((8, 256, 256), BF16),
+            pltpu.VMEM((CHUNKS, PEERS, 64, 128), BF16),
             pltpu.VMEM((CHUNKS, 8, 8, 16, N_DEG), BF16),
             pltpu.VMEM((8, 256, N_DEG), BF16),
             pltpu.VMEM((8, N_DEG, 256), BF16),
@@ -482,7 +505,7 @@
             pltpu.VMEM((CHUNKS, PEERS, 4, 16, 128), BF16),
             pltpu.VMEM((CHUNKS, 8, 128, 256), BF16),
             pltpu.VMEM((2, 1024, 128), F32),
-            pltpu.VMEM((512, 256), F32),
+            pltpu.VMEM((512, 512), F32),
             pltpu.VMEM((2, 8, 256, 128), BF16),
             pltpu.VMEM((CHUNKS, 8, 256, 128), BF16),
             pltpu.VMEM((2, 2, 8, 256, 128), BF16),
@@ -491,7 +514,7 @@
             dma((CHUNKS,)), dma((CHUNKS, 8)), dma, dma, dma((2,)),
             dma((CHUNKS,)), dma((CHUNKS,)), dma((CHUNKS,)), dma((CHUNKS,)),
             dma((CHUNKS,)), dma((CHUNKS, 2)), dma((CHUNKS,)), dma((CHUNKS, 2, 2)),
-            dma((CHUNKS,)), dma((CHUNKS,)),
+            dma((CHUNKS,)), dma((CHUNKS,)), dma, dma, dma,
         ],
         compiler_params=pltpu.CompilerParams(
             collective_id=0, has_side_effects=True, vmem_limit_bytes=62 * 1024 * 1024
@@ -499,18 +522,11 @@
         cost_estimate=pl.CostEstimate(
             flops=17_000_000_000, bytes_accessed=24_000_000, transcendentals=0
         ),
-    )(ent, legendre, quad_weights.reshape(8, 128), azimuthal_orders, azimuthal_flow)
-    updated = pl.pallas_call(
-        radial_kernel,
-        out_shape=jax.ShapeDtypeStruct((8, 256, 512), BF16),
-        in_specs=[vmem, vmem],
-        out_specs=vmem,
-        compiler_params=pltpu.CompilerParams(vmem_limit_bytes=32 * 1024 * 1024),
-        cost_estimate=pl.CostEstimate(
-            flops=3_200_000_000, bytes_accessed=6_000_000, transcendentals=0
-        ),
-    )(received, radial_inverses)
-    return jnp.transpose(updated.reshape(8, 256, 2, 256), (1, 0, 2, 3))
+    )(
+        ent, legendre, quad_weights.reshape(8, 128), azimuthal_orders, azimuthal_flow,
+        radial_inverses,
+    )
+    return jnp.transpose(updated.reshape(8, 2, 256, 256), (2, 0, 1, 3))
 
 
 def solution(mesh):

time: 197 us -> 177 us (0.90)
  local copies, waits for them, and re-layouts: 17 us -> 5.07 us
  Pallas kernels: 179 us -> 171 us
    reshape x5 -> x1, local copies, waits for them, and re-layouts: 15.4 us -> 5.07 us  [shards(): return jnp.transpose(updated.reshape(8, 2, 256, 256), (2, 0, 1, 3))]
    pallas_call x2 -> x1, Pallas kernels: 179 us -> 171 us  [shards(): pl.pallas_call(kernel, out_shape=jax.ShapeDtypeStruct((8, 512, 256), BF16...]
where the time goes in v3:
time: 177 us; the launch traced here: 176 us
  Pallas kernels  171 us (97%)
  local copies, waits for them, and re-layouts  5.07 us (3%)
    pallas_call x1, Pallas kernels, shards(): pl.pallas_call(kernel, out_shape=jax.ShapeDtypeStruct((8, 512, 256), BF16...  171 us
    reshape x1, local copies, waits for them, and re-layouts, shards(): return jnp.transpose(updated.reshape(8, 2, 256, 256), (2, 0, 1, 3))  5.07 us

profile of v3, /device:TPU:1, one launch (start us, length us, event | category | flops | bytes accessed | tf_op | source)
XLA Modules:
  0.0 176.5 jit_solution(13642769240953457550)
XLA Ops:
  0.0 171.4 %shard_map.64 = bf16[8,512,256]{2,1,0:T(8,128)(2,1)} custom-call(bf16[16,64,1024]{2,1,0:T(8,128)(2,1)} %bitcast.9, bf16[16,128,1024]{2,1,0:T(8,128)(2,1)} %leg.1, f32[8,128]{1,0:T(8,128)} %bitcast.10, s32[256]{0:T(256)} %orders.1, bf16[3072,16,128]{2,1,0:T(8,128)(2,1)} %flow.1, bf16[8,256,256]{2,1,0:T(8,128)(2,1)} %inverses.1), custom_call_target="tpu_custom_call" | custom-call | flops 16999999488 | bytes 24000000 | tf_op jit(solution)/shard_map/pallas_call | solution.py:485
  171.4 5.1 %copy.9 = bf16[8,2,256,256]{3,1,0,2:T(2,128)(2,1)} copy(bf16[8,2,256,256]{3,2,1,0:T(8,128)(2,1)} %bitcast.8) | data formatting | bytes 4194304 | tf_op jit(solution)/shard_map/reshape | solution.py:529

commit v4 on v3

--- a/solution.py
+++ b/solution.py
@@ -14,8 +14,18 @@
 PEERS = 32
 CHUNKS = 4
 NT = (((1,), (1,)), ((), ()))
-KB = 256
-FB = 64
+KB = 512
+FB = 128
+ORDER = (
+    "D0", "X", "D1", "M", "F0", "T", "F1", "P", "S0", "D2", "D3", "S1", "G0", "F2", "G1", "F3",
+    "A0", "S2", "S3", "A1", "B0", "G2", "B1", "G3", "V", "A2", "Y0", "Z0", "Y1", "Z1", "B2", "A3",
+    "Y2", "Z2", "B3", "E", "Y3", "Z3",
+)
+
+
+def halves(values):
+    high = values.astype(BF16)
+    return high, (values - high.astype(F32)).astype(BF16)
 
 
 def wait_bytes(ref, sem):
@@ -38,8 +48,8 @@
 
 
 def kernel(
-    ent, leg, qw, orders, flow, inverses, out,
-    er, inv, fr, ef, lg, wt, slope_t, fourier_t, fl, raw, tb, gsend, grecv, msend, mrecv, mx, wide, macc,
+    ent, leg, qw, orders, order_lanes, flow, inverses, out,
+    er, inv, fr, ef, lg, wt, slope_t, fourier_t, fl, tb, gsend, grecv, msend, mrecv, mx, pre, wide, macc,
     r1send, r1recv, r2send, r2recv, fsend,
     ag_send, ag_recv, lg_send, lg_recv, raw_sem, g_send, g_recv, m_send, m_recv,
     r1_ssem, r1_rsem, r2_ssem, r2_rsem, f_send, f_recv, er_sem, inv_sem, out_sem,
@@ -54,13 +64,14 @@
         return (2 * y + index % 2, index // 2)
 
     def raw_copy(block):
-        rows = pl.ds(pl.multiple_of(FB * block, FB), FB)
-        return pltpu.make_async_copy(flow.at[rows], raw.at[block % 2], raw_sem.at[block % 2])
+        pieces = flow.at[pl.ds(FB // 16 * block, FB // 16)]
+        place = r2send.at[block % 4 // 2, block % 2]
+        return pltpu.make_async_copy(pieces, place, raw_sem.at[block % 4])
 
     own_rows = pltpu.make_async_copy(ent, er, er_sem)
     own_rows.start()
-    raw_copy(0).start()
-    raw_copy(1).start()
+    for block in range(4):
+        raw_copy(block).start()
     own_inverses = pltpu.make_async_copy(inverses, inv, inv_sem)
     own_inverses.start()
 
@@ -149,10 +160,17 @@
             gather_wait(j, block)
 
     columns = lax.broadcasted_iota(jnp.int32, (1, 512), 1)
-    column_slots = (columns // 16) * 8 + columns % 8
-
-    def column_order(slot, row):
-        return jnp.where(column_slots == slot, orders[slot].astype(F32), row)
+
+    def order_row():
+        wide_columns = lax.broadcasted_iota(jnp.int32, (256, 512), 1)
+        slots = wide_columns // 16 * 8 + wide_columns % 8
+        hits = (lax.broadcasted_iota(jnp.int32, (256, 512), 0) == slots).astype(F32).astype(BF16)
+        held = jnp.concatenate([order_lanes[0:1, :], order_lanes[1:2, :]], axis=1).astype(F32)
+        held = jnp.broadcast_to(held, (8, 256))
+        high = jnp.floor(held * (1 / 32))
+        low = held - 32.0 * high
+        row = 32.0 * jnp.dot(high.astype(BF16), hits, preferred_element_type=F32)
+        return (row + jnp.dot(low.astype(BF16), hits, preferred_element_type=F32))[0:1, :]
 
     def slope_rows(m_row):
         quarter = jnp.where(columns % 16 >= 8, N_PHI / 4, 0.0)
@@ -189,41 +207,53 @@
 
     def turn_flow(block, carry):
         raw_copy(block).wait()
-        piece = raw[block % 2].reshape(2, FB * 8, 128)
+        piece = r2send[block % 4 // 2, block % 2].reshape(2, 1024, 128)
         for half in range(2):
-            wide[half, : FB * 8, :] = piece[half].astype(F32)
-
-        @pl.when(block + 2 < N_PHI // FB)
+            wide[half] = piece[half].astype(F32)
+
+        @pl.when(block + 4 < N_PHI // FB)
         def _():
-            raw_copy(block + 2).start()
+            raw_copy(block + 4).start()
 
         for half in range(2):
-            rows = pl.ds(pl.multiple_of(FB * block + FB // 2 * half, FB // 2), FB // 2)
+            rows = pl.ds(pl.multiple_of(FB * block + 64 * half, 64), 64)
             for level in range(16):
-                fl[level, rows, :] = wide[half, pl.ds(level, FB // 2, stride=16), :].astype(BF16)
+                fl[level, rows, :] = wide[half, pl.ds(level, 64, stride=16), :].astype(BF16)
         return carry
 
-    def mask(slot, carry):
+    def prepare(slot, carry):
         order = orders[16 * lat + 8 * c + slot]
-        table = lg[slot]
-        degrees = lax.broadcasted_iota(jnp.int32, table.shape, 1)
-        lg[slot] = jnp.where(degrees >= order, table, jnp.zeros_like(table))
-        return carry
-
-    def weigh(slot, carry):
         weights = jnp.concatenate([qw[pl.ds(2 * y, 1), :], qw[pl.ds(2 * y + 1, 1), :]], axis=1)
-        weighted = (jnp.transpose(lg[slot].astype(F32)) * weights).astype(BF16)
         for quarter in range(4):
+            block = jnp.transpose(lg[slot, :, 256 * quarter : 256 * quarter + 256].astype(F32))
+            degrees = lax.broadcasted_iota(jnp.int32, block.shape, 0) + 256 * quarter
+            block = jnp.where(degrees >= order, block, 0.0)
+            lg[slot, :, 256 * quarter : 256 * quarter + 256] = block.astype(BF16)
             rows = pl.ds(pl.multiple_of(256 * ((quarter - y + 4) % 4), 256), 256)
-            wt[slot, rows, :] = weighted[256 * quarter : 256 * quarter + 256]
+            wt[slot, rows, :] = (block * weights).astype(BF16)
         return carry
 
     def synthesize(j):
         gather_rest(j)
+        lanes = pl.ds(pl.multiple_of(256 * y, 256), 256)
+        eye = (
+            lax.broadcasted_iota(jnp.int32, (256, 256), 0)
+            == lax.broadcasted_iota(jnp.int32, (256, 256), 1)
+        ).astype(F32).astype(BF16)
 
         def one(slot, carry):
-            coeffs = ef[j, :, slot].reshape(128, N_DEG)
-            values = lax.dot_general(coeffs, lg[slot], NT, preferred_element_type=F32)
+            values = jnp.zeros((128, 256), F32)
+            for quarter in range(4):
+                span = pl.ds(256 * quarter, 256)
+                values += jnp.dot(
+                    ef[j, :, slot, :, span].reshape(128, 256), lg[slot, :, span],
+                    preferred_element_type=F32,
+                )
+            own = ef[j, :, slot, :, lanes].astype(F32)
+            own = jnp.concatenate([own[:, :8], own[:, 8:]], axis=0).reshape(128, 256)
+            pre[j, slot] = lax.dot_general(
+                eye, own.astype(BF16), NT, preferred_element_type=F32
+            ).astype(BF16)
             for block in range(8):
                 for part in range(2):
                     at = 16 * block + 8 * part
@@ -300,7 +330,7 @@
                         [jnp.concatenate(pieces, axis=1) for pieces in tiles], axis=0
                     )
                     at = 64 * part + 8 * block
-                    mx[j, slot, at : at + 16, :] = both.astype(BF16)
+                    mx[slot, at : at + 16, :] = both.astype(BF16)
             return carry
 
         lax.fori_loop(0, 8, one, 0)
@@ -312,12 +342,13 @@
             wait_bytes(r2send.at[buf], r2_ssem.at[j - 2])
 
         def foreign(slot, carry):
-            sums = lax.dot_general(
-                wt[slot, 256:, :], mx[j, slot], NT, preferred_element_type=F32
-            ).astype(BF16)
-            r2send[buf, 0, slot] = sums[:256]
-            r1send[buf, slot] = sums[256:512]
-            r2send[buf, 1, slot] = sums[512:]
+            sums = lax.dot_general(wt[slot], mx[slot], NT, preferred_element_type=F32)
+            rows = pl.ds(pl.multiple_of(256 * slot, 256), 256)
+            own = sums[:256] + pre[j, slot].astype(F32)
+            pre[j, slot], fl[4 * j, rows, :] = halves(own)
+            r2send[buf, 0, slot], fl[4 * j + 1, rows, :] = halves(sums[256:512])
+            r1send[buf, slot] = sums[512:768].astype(BF16)
+            r2send[buf, 1, slot], fl[4 * j + 2, rows, :] = halves(sums[768:])
             return carry
 
         lax.fori_loop(0, 8, foreign, 0)
@@ -327,74 +358,86 @@
                 r1send.at[buf, span], r1recv.at[j, span],
                 r1_ssem.at[j], r1_rsem.at[j, half], (2 * row + c, lat),
             )
-        reduce_send(j, 0, up, 1)
-        reduce_send(j, 1, down, 0)
-
-    def reduce_send(j, way, row, half):
-        span = pl.ds(4 * half, 4)
+        for part in range(2):
+            reduce_send(j, 0, up, 1, part)
+            reduce_send(j, 1, down, 0, part)
+
+    def reduce_send(j, way, row, half, part):
+        span, rows = pl.ds(4 * half, 4), pl.ds(128 * part, 128)
         remote(
-            r2send.at[j % 2, way, span], r2recv.at[j, way, span],
-            r2_ssem.at[j], r2_rsem.at[j, way, half], (2 * row + c, lat),
+            r2send.at[j % 2, way, span, rows, :], r2recv.at[j, way, span, rows, :],
+            r2_ssem.at[j], r2_rsem.at[j, way, half, part], (2 * row + c, lat),
         )
 
     def reduce_second(j):
-        for way, row, half in ((0, up, 0), (1, down, 1)):
-            span = pl.ds(4 * half, 4)
-            wait_bytes(r1recv.at[j, span], r1_rsem.at[j, half])
-
-            def near(slot, carry):
-                total = r2send[j % 2, way, slot].astype(F32) + r1recv[j, slot].astype(F32)
-                r2send[j % 2, way, slot] = total.astype(BF16)
-                return carry
-
-            lax.fori_loop(4 * half, 4 * half + 4, near, 0)
-            reduce_send(j, way, row, half)
-
-    def finish(j):
+        for half in range(2):
+            wait_bytes(r1recv.at[j, pl.ds(4 * half, 4)], r1_rsem.at[j, half])
+        for part in range(2):
+            rows = pl.ds(128 * part, 128)
+            for way, row, half in ((0, up, 0), (1, down, 1)):
+
+                def near(slot, carry):
+                    lows = pl.ds(pl.multiple_of(256 * slot + 128 * part, 128), 128)
+                    total = r2send[j % 2, way, slot, rows, :].astype(F32)
+                    total += fl[4 * j + 1 + way, lows, :].astype(F32)
+                    total += r1recv[j, slot, rows, :].astype(F32)
+                    r2send[j % 2, way, slot, rows, :] = total.astype(BF16)
+                    return carry
+
+                lax.fori_loop(4 * half, 4 * half + 4, near, 0)
+                reduce_send(j, way, row, half, part)
+
+    def finish(j, part):
         buf = j % 2
+        rows = pl.ds(128 * part, 128)
         for way in range(2):
             for half in range(2):
                 span = pl.ds(4 * half, 4)
-                wait_bytes(r2recv.at[j, way, span], r2_rsem.at[j, way, half])
-        lanes = pl.ds(pl.multiple_of(256 * y, 256), 256)
-        eye = (
-            lax.broadcasted_iota(jnp.int32, (256, 256), 0)
-            == lax.broadcasted_iota(jnp.int32, (256, 256), 1)
-        ).astype(F32).astype(BF16)
+                wait_bytes(r2recv.at[j, way, span, rows, :], r2_rsem.at[j, way, half, part])
 
         def one(slot, carry):
-            own = ef[j, :, slot, :, lanes].astype(F32)
-            own = jnp.concatenate([own[:, :8], own[:, 8:]], axis=0).reshape(128, 256)
-            total = lax.dot_general(
-                wt[slot, :256, :], mx[j, slot], NT, preferred_element_type=F32
-            ) + lax.dot_general(eye, own.astype(BF16), NT, preferred_element_type=F32)
-            total += r2recv[j, 0, slot].astype(F32) + r2recv[j, 1, slot].astype(F32)
-            for core in range(2):
-                for p in range(16):
-                    at = 128 * core + 8 * p
-                    wide[core, pl.ds(64 * p + slot, 8, stride=8), :] = total[at : at + 8]
+            lows = pl.ds(pl.multiple_of(256 * slot + 128 * part, 128), 128)
+            total = pre[j, slot, rows, :].astype(F32) + fl[4 * j, lows, :].astype(F32)
+            total += r2recv[j, 0, slot, rows, :].astype(F32)
+            total += r2recv[j, 1, slot, rows, :].astype(F32)
+            for p in range(16):
+                wide[part, pl.ds(64 * p + slot, 8, stride=8), :] = total[8 * p : 8 * p + 8]
             return carry
 
         lax.fori_loop(0, 8, one, 0)
-        if j >= 2:
+        if j >= 2 and part == 0:
             sent(fsend.at[buf], f_send.at[j - 2])
-            wait_bytes(fr.at[j - 2], f_recv.at[j - 2])
+            if j == 2:
+                wait_bytes(fr.at[0], f_recv.at[0])
 
         def pack(p, carry):
-            rows = pl.ds(pl.multiple_of(64 * p, 64), 64)
-            for core in range(2):
-                fsend[buf, 2 * p + core] = wide[core, rows, :].astype(BF16)
+            span = pl.ds(pl.multiple_of(64 * p, 64), 64)
+            fsend[buf, 2 * p + part] = wide[part, span, :].astype(BF16)
             return carry
 
         lax.fori_loop(0, 16, pack, 0)
-        all_to_all(lambda dest: fsend.at[buf, dest], fr.at[j, me], f_send.at[j], f_recv.at[j])
-
-    gather_direct(0)
-    mine = pl.ds(pl.multiple_of(128 * c, 128), 128)
-    remote(
-        leg.at[pl.ds(8 * (1 - c), 8)], lg.at[:, mine, :], lg_send, lg_recv, (2 * y + 1 - c, lat)
-    )
-    pltpu.make_async_copy(leg.at[pl.ds(8 * c, 8)], lg.at[:, mine, :], lg_recv).start()
+
+        def send(offset, carry):
+            p = (lat + offset) % 16
+            remote(
+                fsend.at[buf, 2 * p + part], fr.at[j, me],
+                f_send.at[j], f_recv.at[j], (2 * y + part, p),
+            )
+            return carry
+
+        lax.fori_loop(1, 16, send, 0)
+
+        @pl.when(c == part)
+        def _():
+            pltpu.make_async_copy(fsend.at[buf, me], fr.at[j, me], f_recv.at[j]).start()
+
+        @pl.when(c != part)
+        def _():
+            remote(
+                fsend.at[buf, 2 * lat + part], fr.at[j, me],
+                f_send.at[j], f_recv.at[j], (2 * y + part, lat),
+            )
+
     def spread(degree, carry):
         source = lax.broadcasted_iota(jnp.int32, (256, 512), 0)
         lane = lax.broadcasted_iota(jnp.int32, (256, 512), 1)
@@ -406,73 +449,95 @@
     def out_copy(degree):
         return pltpu.make_async_copy(wt.at[degree, pl.ds(0, 512), :], out.at[degree], out_sem)
 
-    def radial(index, carry):
-        rows = pl.ds(pl.multiple_of(16 * index, 16), 16)
-        part = lax.broadcasted_iota(jnp.int32, (256, 512), 1) % 128 // 64
-        piece = fr[:, :, rows, :].astype(F32)
+    def update(chunks, degree_pair, store):
+        rows = pl.ds(pl.multiple_of(16 * degree_pair, 16), 16)
+        width = 128 * len(chunks)
+        part = lax.broadcasted_iota(jnp.int32, (256, width), 1) % 128 // 64
+        pieces = [fr[j, :, rows, :].astype(F32) for j in chunks]
         for u in range(2):
-            flat = piece[:, :, 8 * u : 8 * u + 8, :].reshape(CHUNKS, 256, 128)
-            left = jnp.concatenate([flat[j] for j in range(CHUNKS)], axis=1)
-            degree = 2 * index + u
+            flat = [piece[:, 8 * u : 8 * u + 8, :].reshape(256, 128) for piece in pieces]
+            left = jnp.concatenate(flat, axis=1)
+            degree = 2 * degree_pair + u
             for half in range(2):
-                wt[degree, 256 * half : 256 * half + 256, :] = lax.dot_general(
-                    jnp.where(part == half, left, 0.0).astype(BF16), lg[degree, :, :512], NT,
+                right = lg[degree, :, 128 * chunks[0] : 128 * chunks[0] + width]
+                store(degree, half, lax.dot_general(
+                    jnp.where(part == half, left, 0.0).astype(BF16), right, NT,
                     preferred_element_type=F32,
-                ).astype(BF16)
-            out_copy(degree).start()
+                ))
+
+    def early(degree_pair, carry):
+        def store(degree, half, values):
+            rows = pl.ds(pl.multiple_of(256 * degree, 256), 256)
+            span = pl.ds(256 * half, 256)
+            lg[degree, :, pl.ds(512 + 256 * half, 256)], slope_t[rows, span] = halves(values)
+
+        update((0, 1, 2), degree_pair, store)
         return carry
 
-    gather_direct(1)
-    wait_bytes(lg, lg_recv)
-    lax.fori_loop(0, 8, mask, 0)
-    lax.fori_loop(0, 8, weigh, 0)
-    gather_forward(0)
-    lax.fori_loop(0, N_PHI // FB, turn_flow, 0)
-    gather_forward(1)
-    m_row = lax.fori_loop(0, 256, column_order, jnp.zeros((1, 512), F32))
-    slope_rows(m_row)
-    fourier_rows(m_row)
-    synthesize(0)
-    gather_direct(2)
-    gather_direct(3)
-    synthesize(1)
-    grid(0)
-    gather_forward(2)
-    grid(1)
-    gather_forward(3)
-    arrange(0)
-    reduce_first(0)
-    synthesize(2)
-    synthesize(3)
-    arrange(1)
-    reduce_first(1)
-    reduce_second(0)
-    grid(2)
-    reduce_second(1)
-    grid(3)
-    own_inverses.wait()
-    lax.fori_loop(0, 8, spread, 0)
-    arrange(2)
-    reduce_first(2)
-    finish(0)
-    finish(1)
-    reduce_second(2)
-    arrange(3)
-    reduce_first(3)
-    finish(2)
-    reduce_second(3)
-    finish(3)
+    def late(degree_pair, carry):
+        def store(degree, half, values):
+            rows = pl.ds(pl.multiple_of(256 * degree, 256), 256)
+            values += lg[degree, :, 512 + 256 * half : 768 + 256 * half].astype(F32)
+            values += slope_t[rows, 256 * half : 256 * half + 256].astype(F32)
+            wt[degree, 256 * half : 256 * half + 256, :] = values.astype(BF16)
+
+        update((3,), degree_pair, store)
+        for u in range(2):
+            out_copy(2 * degree_pair + u).start()
+        return carry
+
+    def prepare_legendre():
+        wait_bytes(lg, lg_recv)
+        lax.fori_loop(0, 8, prepare, 0)
+
+    def prepare_flow():
+        lax.fori_loop(0, N_PHI // FB, turn_flow, 0)
+
+    def prepare_tables():
+        m_row = order_row()
+        slope_rows(m_row)
+        fourier_rows(m_row)
+
+    def prepare_inverses():
+        own_inverses.wait()
+        lax.fori_loop(0, 8, spread, 0)
+
+    def begin_radial():
+        for j in (1, 2):
+            wait_bytes(fr.at[j], f_recv.at[j])
+        lax.fori_loop(0, 4, early, 0)
+
+    def swap_tables():
+        mine = pl.ds(pl.multiple_of(128 * c, 128), 128)
+        remote(
+            leg.at[pl.ds(8 * (1 - c), 8)], lg.at[:, mine, :], lg_send, lg_recv,
+            (2 * y + 1 - c, lat),
+        )
+        pltpu.make_async_copy(leg.at[pl.ds(8 * c, 8)], lg.at[:, mine, :], lg_recv).start()
+
+    steps = dict(
+        D=gather_direct, F=gather_forward, S=synthesize, G=grid, B=reduce_second,
+        X=swap_tables, M=prepare_legendre, T=prepare_flow, P=prepare_tables,
+        V=prepare_inverses, E=begin_radial, Y=lambda j: finish(j, 0), Z=lambda j: finish(j, 1),
+    )
+    for step in ORDER:
+        if step[0] == "A":
+            arrange(int(step[1]))
+            reduce_first(int(step[1]))
+        else:
+            steps[step[0]](*(int(digit) for digit in step[1:]))
+
     for j in range(CHUNKS):
         wait_bytes(ef.at[j, pl.ds(0, 7)], ag_send.at[j])
+    wait_bytes(lg.at[:, pl.ds(0, 128), :], lg_send)
     for j in range(CHUNKS - 2, CHUNKS):
         sent(gsend.at[j % 2], g_send.at[j])
         sent(msend.at[j % 2], m_send.at[j])
         wait_bytes(r1send.at[j % 2], r1_ssem.at[j])
         wait_bytes(r2send.at[j % 2], r2_ssem.at[j])
         sent(fsend.at[j % 2], f_send.at[j])
-        wait_bytes(fr.at[j], f_recv.at[j])
-    wait_bytes(lg.at[:, pl.ds(0, 128), :], lg_send)
-    lax.fori_loop(0, 4, radial, 0)
+    wait_bytes(fr.at[3], f_recv.at[3])
+    lax.fori_loop(0, 4, late, 0)
     wait_bytes(wt.at[:, pl.ds(0, 512), :], out_sem)
 
 
@@ -485,7 +550,7 @@
     updated = pl.pallas_call(
         kernel,
         out_shape=jax.ShapeDtypeStruct((8, 512, 256), BF16),
-        in_specs=[hbm, hbm, vmem, smem, hbm, hbm],
+        in_specs=[hbm, hbm, vmem, smem, vmem, hbm, hbm],
         out_specs=hbm,
         scratch_shapes=[
             pltpu.VMEM((16, 64, N_DEG), BF16),
@@ -497,13 +562,13 @@
             pltpu.VMEM((N_PHI, 512), BF16),
             pltpu.VMEM((512, N_PHI), BF16),
             pltpu.VMEM((16, N_PHI, 128), BF16),
-            pltpu.VMEM((2, FB, 16, 128), BF16),
             pltpu.VMEM((2, 64, 512), F32),
             pltpu.VMEM((2, PEERS, 4, 16, 128), BF16),
             pltpu.VMEM((CHUNKS, 4, 512, 128), BF16),
             pltpu.VMEM((2, PEERS, 4, 16, 128), BF16),
             pltpu.VMEM((CHUNKS, PEERS, 4, 16, 128), BF16),
-            pltpu.VMEM((CHUNKS, 8, 128, 256), BF16),
+            pltpu.VMEM((8, 128, 256), BF16),
+            pltpu.VMEM((CHUNKS, 8, 256, 128), BF16),
             pltpu.VMEM((2, 1024, 128), F32),
             pltpu.VMEM((512, 512), F32),
             pltpu.VMEM((2, 8, 256, 128), BF16),
@@ -511,9 +576,9 @@
             pltpu.VMEM((2, 2, 8, 256, 128), BF16),
             pltpu.VMEM((CHUNKS, 2, 8, 256, 128), BF16),
             pltpu.VMEM((2, PEERS, 64, 128), BF16),
-            dma((CHUNKS,)), dma((CHUNKS, 8)), dma, dma, dma((2,)),
+            dma((CHUNKS,)), dma((CHUNKS, 8)), dma, dma, dma((4,)),
             dma((CHUNKS,)), dma((CHUNKS,)), dma((CHUNKS,)), dma((CHUNKS,)),
-            dma((CHUNKS,)), dma((CHUNKS, 2)), dma((CHUNKS,)), dma((CHUNKS, 2, 2)),
+            dma((CHUNKS,)), dma((CHUNKS, 2)), dma((CHUNKS,)), dma((CHUNKS, 2, 2, 2)),
             dma((CHUNKS,)), dma((CHUNKS,)), dma, dma, dma,
         ],
         compiler_params=pltpu.CompilerParams(
@@ -523,7 +588,8 @@
             flops=17_000_000_000, bytes_accessed=24_000_000, transcendentals=0
         ),
     )(
-        ent, legendre, quad_weights.reshape(8, 128), azimuthal_orders, azimuthal_flow,
+        ent, legendre, quad_weights.reshape(8, 128), azimuthal_orders,
+        azimuthal_orders.reshape(2, 128), azimuthal_flow.reshape(N_PHI // 16, 256, 128),
         radial_inverses,
     )
     return jnp.transpose(updated.reshape(8, 2, 256, 256), (2, 0, 1, 3))

time: 177 us -> 163 us (0.921)
  Pallas kernels: 171 us -> 157 us
    pallas_call x1, Pallas kernels: 171 us -> 157 us  [shards(): pl.pallas_call(kernel, out_shape=jax.ShapeDtypeStruct((8, 512, 256), BF16...]
where the time goes in v4:
time: 163 us; the launch traced here: 162 us
  Pallas kernels  157 us (96%)
  local copies, waits for them, and re-layouts  5.07 us (3%)
    pallas_call x1, Pallas kernels, shards(): pl.pallas_call(kernel, out_shape=jax.ShapeDtypeStruct((8, 512, 256), BF16...  157 us
    reshape x1, local copies, waits for them, and re-layouts, shards(): return jnp.transpose(updated.reshape(8, 2, 256, 256), (2, 0, 1, 3))  5.07 us

profile of v4, /device:TPU:1, one launch (start us, length us, event | category | flops | bytes accessed | tf_op | source)
XLA Modules:
  0.0 162.4 jit_solution(1333302490543832287)
XLA Ops:
  0.0 157.3 %shard_map.64 = bf16[8,512,256]{2,1,0:T(8,128)(2,1)} custom-call(bf16[16,64,1024]{2,1,0:T(8,128)(2,1)} %bitcast.12, bf16[16,128,1024]{2,1,0:T(8,128)(2,1)} %leg.1, f32[8,128]{1,0:T(8,128)} %bitcast.13, s32[256]{0:T(256)} %orders.1, s32[2,128]{1,0:T(2,128)} %bitcast.14, bf16[192,256,128]{2,1,0:T(8,128)(2,1)} %bitcast.11, bf16[8,256,256]{2,1,0:T(8,128)(2,1)} %inverses.1), custom_call_target="tpu_custom_call" | custom-call | flops 16999999488 | bytes 24000000 | tf_op jit(solution)/shard_map/pallas_call | solution.py:550
  157.3 5.1 %copy.9 = bf16[8,2,256,256]{3,1,0,2:T(2,128)(2,1)} copy(bf16[8,2,256,256]{3,2,1,0:T(8,128)(2,1)} %bitcast.10) | data formatting | bytes 4194304 | tf_op jit(solution)/shard_map/reshape | solution.py:595

commit v5 on v4

--- a/solution.py
+++ b/solution.py
@@ -16,10 +16,12 @@
 NT = (((1,), (1,)), ((), ()))
 KB = 512
 FB = 128
+PARTS = 4
+ROWS = 256 // PARTS
 ORDER = (
     "D0", "X", "D1", "M", "F0", "T", "F1", "P", "S0", "D2", "D3", "S1", "G0", "F2", "G1", "F3",
-    "A0", "S2", "S3", "A1", "B0", "G2", "B1", "G3", "V", "A2", "Y0", "Z0", "Y1", "Z1", "B2", "A3",
-    "Y2", "Z2", "B3", "E", "Y3", "Z3",
+    "A0", "S2", "S3", "A1", "B0", "G2", "B1", "G3", "V", "A2", "Z00", "Z01", "Z02", "Z03", "Z10",
+    "Z11", "Z12", "Z13", "B2", "A3", "Z20", "Z21", "Z22", "Z23", "B3", "Z30", "Z31", "Z32", "Z33", "E",
 )
 
 
@@ -358,12 +360,12 @@
                 r1send.at[buf, span], r1recv.at[j, span],
                 r1_ssem.at[j], r1_rsem.at[j, half], (2 * row + c, lat),
             )
-        for part in range(2):
+        for part in range(PARTS):
             reduce_send(j, 0, up, 1, part)
             reduce_send(j, 1, down, 0, part)
 
     def reduce_send(j, way, row, half, part):
-        span, rows = pl.ds(4 * half, 4), pl.ds(128 * part, 128)
+        span, rows = pl.ds(4 * half, 4), pl.ds(ROWS * part, ROWS)
         remote(
             r2send.at[j % 2, way, span, rows, :], r2recv.at[j, way, span, rows, :],
             r2_ssem.at[j], r2_rsem.at[j, way, half, part], (2 * row + c, lat),
@@ -372,12 +374,12 @@
     def reduce_second(j):
         for half in range(2):
             wait_bytes(r1recv.at[j, pl.ds(4 * half, 4)], r1_rsem.at[j, half])
-        for part in range(2):
-            rows = pl.ds(128 * part, 128)
+        for part in range(PARTS):
+            rows = pl.ds(ROWS * part, ROWS)
             for way, row, half in ((0, up, 0), (1, down, 1)):
 
                 def near(slot, carry):
-                    lows = pl.ds(pl.multiple_of(256 * slot + 128 * part, 128), 128)
+                    lows = pl.ds(pl.multiple_of(256 * slot + ROWS * part, ROWS), ROWS)
                     total = r2send[j % 2, way, slot, rows, :].astype(F32)
                     total += fl[4 * j + 1 + way, lows, :].astype(F32)
                     total += r1recv[j, slot, rows, :].astype(F32)
@@ -388,55 +390,51 @@
                 reduce_send(j, way, row, half, part)
 
     def finish(j, part):
-        buf = j % 2
-        rows = pl.ds(128 * part, 128)
+        buf, core, first = j % 2, part * 2 // PARTS, part % (PARTS // 2) * (32 // PARTS)
+        rows = pl.ds(ROWS * part, ROWS)
         for way in range(2):
             for half in range(2):
                 span = pl.ds(4 * half, 4)
                 wait_bytes(r2recv.at[j, way, span, rows, :], r2_rsem.at[j, way, half, part])
 
         def one(slot, carry):
-            lows = pl.ds(pl.multiple_of(256 * slot + 128 * part, 128), 128)
+            lows = pl.ds(pl.multiple_of(256 * slot + ROWS * part, ROWS), ROWS)
             total = pre[j, slot, rows, :].astype(F32) + fl[4 * j, lows, :].astype(F32)
             total += r2recv[j, 0, slot, rows, :].astype(F32)
             total += r2recv[j, 1, slot, rows, :].astype(F32)
-            for p in range(16):
-                wide[part, pl.ds(64 * p + slot, 8, stride=8), :] = total[8 * p : 8 * p + 8]
+            for p in range(32 // PARTS):
+                at = 64 * (first + p) + slot
+                wide[core, pl.ds(at, 8, stride=8), :] = total[8 * p : 8 * p + 8]
             return carry
 
         lax.fori_loop(0, 8, one, 0)
         if j >= 2 and part == 0:
             sent(fsend.at[buf], f_send.at[j - 2])
-            if j == 2:
-                wait_bytes(fr.at[0], f_recv.at[0])
+            wait_bytes(fr.at[j - 2], f_recv.at[j - 2])
 
         def pack(p, carry):
             span = pl.ds(pl.multiple_of(64 * p, 64), 64)
-            fsend[buf, 2 * p + part] = wide[part, span, :].astype(BF16)
-            return carry
-
-        lax.fori_loop(0, 16, pack, 0)
+            fsend[buf, 2 * p + core] = wide[core, span, :].astype(BF16)
+            return carry
+
+        lax.fori_loop(first, first + 32 // PARTS, pack, 0)
 
         def send(offset, carry):
-            p = (lat + offset) % 16
-            remote(
-                fsend.at[buf, 2 * p + part], fr.at[j, me],
-                f_send.at[j], f_recv.at[j], (2 * y + part, p),
-            )
-            return carry
-
-        lax.fori_loop(1, 16, send, 0)
-
-        @pl.when(c == part)
-        def _():
-            pltpu.make_async_copy(fsend.at[buf, me], fr.at[j, me], f_recv.at[j]).start()
-
-        @pl.when(c != part)
-        def _():
-            remote(
-                fsend.at[buf, 2 * lat + part], fr.at[j, me],
-                f_send.at[j], f_recv.at[j], (2 * y + part, lat),
-            )
+            p = first + (lat + offset) % (32 // PARTS)
+            itself = (p == lat) & (c == core)
+            source, target = fsend.at[buf, 2 * p + core], fr.at[j, me]
+
+            @pl.when(itself)
+            def _():
+                pltpu.make_async_copy(source, target, f_recv.at[j]).start()
+
+            @pl.when(jnp.logical_not(itself))
+            def _():
+                remote(source, target, f_send.at[j], f_recv.at[j], (2 * y + core, p))
+
+            return carry
+
+        lax.fori_loop(0, 32 // PARTS, send, 0)
 
     def spread(degree, carry):
         source = lax.broadcasted_iota(jnp.int32, (256, 512), 0)
@@ -503,8 +501,7 @@
         lax.fori_loop(0, 8, spread, 0)
 
     def begin_radial():
-        for j in (1, 2):
-            wait_bytes(fr.at[j], f_recv.at[j])
+        wait_bytes(fr.at[2], f_recv.at[2])
         lax.fori_loop(0, 4, early, 0)
 
     def swap_tables():
@@ -518,7 +515,7 @@
     steps = dict(
         D=gather_direct, F=gather_forward, S=synthesize, G=grid, B=reduce_second,
         X=swap_tables, M=prepare_legendre, T=prepare_flow, P=prepare_tables,
-        V=prepare_inverses, E=begin_radial, Y=lambda j: finish(j, 0), Z=lambda j: finish(j, 1),
+        V=prepare_inverses, E=begin_radial, Z=finish,
     )
     for step in ORDER:
         if step[0] == "A":
@@ -578,7 +575,7 @@
             pltpu.VMEM((2, PEERS, 64, 128), BF16),
             dma((CHUNKS,)), dma((CHUNKS, 8)), dma, dma, dma((4,)),
             dma((CHUNKS,)), dma((CHUNKS,)), dma((CHUNKS,)), dma((CHUNKS,)),
-            dma((CHUNKS,)), dma((CHUNKS, 2)), dma((CHUNKS,)), dma((CHUNKS, 2, 2, 2)),
+            dma((CHUNKS,)), dma((CHUNKS, 2)), dma((CHUNKS,)), dma((CHUNKS, 2, 2, PARTS)),
             dma((CHUNKS,)), dma((CHUNKS,)), dma, dma, dma,
         ],
         compiler_params=pltpu.CompilerParams(

time: 163 us -> 161 us (0.988)
    pallas_call x1, Pallas kernels: 157 us -> 156 us  [shards(): pl.pallas_call(kernel, out_shape=jax.ShapeDtypeStruct((8, 512, 256), BF16...]
where the time goes in v5:
time: 161 us
  Pallas kernels  156 us (97%)
  local copies, waits for them, and re-layouts  5.07 us (3%)
    pallas_call x1, Pallas kernels, shards(): pl.pallas_call(kernel, out_shape=jax.ShapeDtypeStruct((8, 512, 256), BF16...  156 us
    reshape x1, local copies, waits for them, and re-layouts, shards(): return jnp.transpose(updated.reshape(8, 2, 256, 256), (2, 0, 1, 3))  5.07 us

profile of v5, /device:TPU:1, one launch (start us, length us, event | category | flops | bytes accessed | tf_op | source)
XLA Modules:
  0.0 160.6 jit_solution(3266713579123174196)
XLA Ops:
  0.0 155.6 %shard_map.64 = bf16[8,512,256]{2,1,0:T(8,128)(2,1)} custom-call(bf16[16,64,1024]{2,1,0:T(8,128)(2,1)} %bitcast.12, bf16[16,128,1024]{2,1,0:T(8,128)(2,1)} %leg.1, f32[8,128]{1,0:T(8,128)} %bitcast.13, s32[256]{0:T(256)} %orders.1, s32[2,128]{1,0:T(2,128)} %bitcast.14, bf16[192,256,128]{2,1,0:T(8,128)(2,1)} %bitcast.11, bf16[8,256,256]{2,1,0:T(8,128)(2,1)} %inverses.1), custom_call_target="tpu_custom_call" | custom-call | flops 16999999488 | bytes 24000000 | tf_op jit(solution)/shard_map/pallas_call | solution.py:547
  155.6 5.1 %copy.9 = bf16[8,2,256,256]{3,1,0,2:T(2,128)(2,1)} copy(bf16[8,2,256,256]{3,2,1,0:T(8,128)(2,1)} %bitcast.10) | data formatting | bytes 4194304 | tf_op jit(solution)/shard_map/reshape | solution.py:592

commit v6 on v5

--- a/solution.py
+++ b/solution.py
@@ -14,7 +14,7 @@
 PEERS = 32
 CHUNKS = 4
 NT = (((1,), (1,)), ((), ()))
-KB = 512
+KB = 256
 FB = 128
 PARTS = 4
 ROWS = 256 // PARTS

time: 161 us -> 161 us (level)
  no operation moved by 1% of the time
where the time goes in v6:
time: 161 us
  Pallas kernels  156 us (97%)
  local copies, waits for them, and re-layouts  5.07 us (3%)
    pallas_call x1, Pallas kernels, shards(): pl.pallas_call(kernel, out_shape=jax.ShapeDtypeStruct((8, 512, 256), BF16...  156 us
    reshape x1, local copies, waits for them, and re-layouts, shards(): return jnp.transpose(updated.reshape(8, 2, 256, 256), (2, 0, 1, 3))  5.07 us

profile of v6, /device:TPU:1, one launch (start us, length us, event | category | flops | bytes accessed | tf_op | source)
XLA Modules:
  0.0 160.6 jit_solution(15925273097440338584)
XLA Ops:
  0.0 155.6 %shard_map.64 = bf16[8,512,256]{2,1,0:T(8,128)(2,1)} custom-call(bf16[16,64,1024]{2,1,0:T(8,128)(2,1)} %bitcast.12, bf16[16,128,1024]{2,1,0:T(8,128)(2,1)} %leg.1, f32[8,128]{1,0:T(8,128)} %bitcast.13, s32[256]{0:T(256)} %orders.1, s32[2,128]{1,0:T(2,128)} %bitcast.14, bf16[192,256,128]{2,1,0:T(8,128)(2,1)} %bitcast.11, bf16[8,256,256]{2,1,0:T(8,128)(2,1)} %inverses.1), custom_call_target="tpu_custom_call" | custom-call | flops 16999999488 | bytes 24000000 | tf_op jit(solution)/shard_map/pallas_call | solution.py:547
  155.6 5.1 %copy.9 = bf16[8,2,256,256]{3,1,0,2:T(2,128)(2,1)} copy(bf16[8,2,256,256]{3,2,1,0:T(8,128)(2,1)} %bitcast.10) | data formatting | bytes 4194304 | tf_op jit(solution)/shard_map/reshape | solution.py:592
